TPU v7x, 128 devices: a whole 4x4x4 slice. The times are simulated.
128 devices in a mesh: dp: 8 (over y_hi, x), ctx: 16 (over z, y_lo, core).
Axes of the slice: x: 4, y: 4 (y_hi: 2, y_lo: 2; y = y_hi * 2 + y_lo), z: 4, core: 2. Of those that a mesh axis runs over, the one named last changes fastest.
Arguments:
- query: bfloat16 [8, 2048, 4096], P('dp', 'ctx'), may hold values from -6 to 6
- key: bfloat16 [8, 2048, 256], P('dp', 'ctx'), may hold values from -6 to 6
- value: bfloat16 [8, 2048, 256], P('dp', 'ctx'), may hold values from -6 to 6
- span_order: int32 [8, 32], P('dp'), may hold values from 0 to 31, each once within a row
- expert_ids: int32 [8, 2048, 8], P('dp', 'ctx'), may hold values from 0 to 127, as said below
- expert_gates: float32 [8, 2048, 8], P('dp', 'ctx'), may hold values from 0.02 to 0.2
- trainable: int32 [16], replicated, may hold values from 0 to 127, as said below
- norm_gain: float32 [4096], replicated, may hold values from 0.5 to 1.5
- upstream: bfloat16 [8, 2048, 4096], P('dp', 'ctx'), may hold values from -6 to 6
- expert_weights: bfloat16 [16, 768, 3, 4096], P('ctx'), may hold values from -0.09375 to 0.09375
Outputs:
- d_query: bfloat16 [8, 2048, 4096], P('dp', 'ctx')
- key_gradient: bfloat16 [8, 2048, 256], P('dp', 'ctx')
- value_gradient: bfloat16 [8, 2048, 256], P('dp', 'ctx')
- expert_grads: bfloat16 [16, 768, 3, 4096], P('ctx', 'dp')
Inputs may be any that keep to these rules, and one draw needn't show every extreme that they name: `span_order`: each row is a permutation of the 32 span numbers. `expert_ids`: the 8 numbers of a token are distinct; among the 128 rows of one device (aligned blocks of 128 rows of a document) at most 12 name the same expert. `trainable`: distinct expert numbers.
All inputs are finite; a program needn't handle non-finite values.
Results may differ from a plain program's by a relative error of at most 0.02.
Values may be sent and summed in bfloat16 or wider, within the bound.
A program may use at most 128 MiB of HBM per device.

v0:
```python
import math

import jax
import jax.numpy as jnp
from jax import lax
from jax.experimental import pallas as pl
from jax.experimental.pallas import tpu as pltpu
from jax.sharding import PartitionSpec as P

D = 4096
QUERY_HEADS = 32
KEY_VALUE_HEADS = 2
HEAD_SIZE = 128
TOP = 8
CAP = 12
H = 768
N_CTX = 16
N_CHIP = 8
ROWS = 128
KEYS = 2048
SLOTS = 16
FOLDS = 4
WIDE = D // FOLDS
SLAB = CAP * FOLDS
SLAB_ROWS = SLOTS * SLAB
PAIRS = QUERY_HEADS // 2
KEY_BLOCK = 512

MASK_FILLER = -1e30
EPSILON = 1e-06
INV_ROOT = HEAD_SIZE ** (-0.5)
TO_BASE_TWO = INV_ROOT * math.log2(math.e)

MESH = pl.DeviceIdType.MESH
VMEM_LIMIT = 60 * 2**20
BF = jnp.bfloat16
F32 = jnp.float32


def dot_nn(a, b):
    return lax.dot_general(a, b, (((1,), (0,)), ((), ())), preferred_element_type=F32)


def dot_nt(a, b):
    return lax.dot_general(a, b, (((1,), (1,)), ((), ())), preferred_element_type=F32)


def dot_tn(a, b):
    return lax.dot_general(a, b, (((0,), (0,)), ((), ())), preferred_element_type=F32)


def in_vmem(count):
    return [pl.BlockSpec(memory_space=pltpu.VMEM)] * count


def local(cost):
    return dict(
        compiler_params=pltpu.CompilerParams(vmem_limit_bytes=VMEM_LIMIT),
        cost_estimate=pl.CostEstimate(flops=cost, bytes_accessed=2**22, transcendentals=0),
    )


def slot_masks(ids_ref, gates_ref, trainable_ref):
    experts = trainable_ref[...]
    hits = jnp.zeros((SLOTS, ROWS), F32)
    gates = jnp.zeros((SLOTS, ROWS), F32)
    for k in range(TOP):
        same = ids_ref[k : k + 1, :] == experts
        hits = hits + jnp.where(same, 1.0, 0.0)
        gates = gates + jnp.where(same, gates_ref[k : k + 1, :], 0.0)
    before = lax.broadcasted_iota(jnp.int32, (ROWS, ROWS), 0) < lax.broadcasted_iota(
        jnp.int32, (ROWS, ROWS), 1
    )
    rank = dot_nn(hits.astype(BF), jnp.where(before, 1.0, 0.0).astype(BF))
    rank = jnp.where(hits > 0.5, rank, -1.0)
    row = lax.broadcasted_iota(jnp.int32, (SLAB, 1), 0)
    fold = sum(jnp.where(row >= CAP * f, 1, 0) for f in range(1, FOLDS))
    within = (row - CAP * fold).astype(F32)
    masks = [[] for _ in range(FOLDS)]
    row_gate = []
    for j in range(SLOTS):
        match = jnp.broadcast_to(rank[j : j + 1, :], (SLAB, ROWS)) == within
        row_gate.append(
            jnp.sum(jnp.where(match, gates[j : j + 1, :], 0.0), axis=1, keepdims=True)
        )
        for f in range(FOLDS):
            masks[f].append(jnp.where(match & (fold == f), 1.0, 0.0))
    return (
        [jnp.concatenate(m, axis=0).astype(BF) for m in masks],
        jnp.concatenate(row_gate, axis=0),
    )


def fold_of(ref, f):
    return ref[:, f * WIDE : (f + 1) * WIDE]


def unfold_mask(f):
    n = lax.broadcasted_iota(jnp.int32, (SLOTS * CAP, SLAB_ROWS), 0)
    m = lax.broadcasted_iota(jnp.int32, (SLOTS * CAP, SLAB_ROWS), 1)
    source = lax.shift_right_logical(n * 5462, 16)
    return jnp.where(m == n + (SLAB - CAP) * source + CAP * f, 1.0, 0.0).astype(BF)


def refold_mask(f):
    n = lax.broadcasted_iota(jnp.int32, (SLAB_ROWS, SLOTS * CAP), 1)
    m = lax.broadcasted_iota(jnp.int32, (SLAB_ROWS, SLOTS * CAP), 0)
    source = lax.shift_right_logical(n * 5462, 16)
    return jnp.where(m == n + (SLAB - CAP) * source + CAP * f, 1.0, 0.0).astype(BF)


def weighted_kernel(ids_ref, gates_ref, trainable_ref, up_ref, out_ref):
    masks, row_gate = slot_masks(ids_ref, gates_ref, trainable_ref)
    total = dot_nn(masks[0], fold_of(up_ref, 0))
    for f in range(1, FOLDS):
        total = total + dot_nn(masks[f], fold_of(up_ref, f))
    out_ref[...] = (row_gate * total).astype(BF)


def two_heads(ref, pair):
    at = pl.multiple_of(pair * 2 * HEAD_SIZE, 2 * HEAD_SIZE)
    both = ref[:, pl.ds(at, 2 * HEAD_SIZE)]
    return jnp.concatenate([both[:, :HEAD_SIZE], both[:, HEAD_SIZE:]], axis=0)


def put_two_heads(ref, pair, stacked):
    at = pl.multiple_of(pair * 2 * HEAD_SIZE, 2 * HEAD_SIZE)
    ref[:, pl.ds(at, 2 * HEAD_SIZE)] = jnp.concatenate([stacked[:ROWS], stacked[ROWS:]], axis=1)


def diagonal():
    eye = lax.broadcasted_iota(jnp.int32, (ROWS, ROWS), 0) == lax.broadcasted_iota(
        jnp.int32, (ROWS, ROWS), 1
    )
    one = jnp.where(eye, MASK_FILLER, 0.0).astype(BF)
    return jnp.concatenate([one, one], axis=0)


def rms_factor(features):
    return lax.rsqrt(jnp.mean(features * features, axis=1, keepdims=True) + EPSILON)


def forward_kernel(
    q_ref, kv_ref, hidden_ref, ids_ref, gates_ref, trainable_ref, gain_ref,
    mixed_ref, spread_ref, slab_ref,
    masked_keys, values_t, hides, scores,
):
    for g in range(KEY_VALUE_HEADS):
        masked_keys[g, :, :HEAD_SIZE] = kv_ref[:, g * HEAD_SIZE : (g + 1) * HEAD_SIZE]
        masked_keys[g, :, HEAD_SIZE:] = hidden_ref[...]
        at = (KEY_VALUE_HEADS + g) * HEAD_SIZE
        values_t[g] = kv_ref[:, at : at + HEAD_SIZE].T
    hides[...] = diagonal()

    def step(pair, carry):
        g = lax.div(pair, PAIRS // KEY_VALUE_HEADS)
        queries = jnp.concatenate([two_heads(q_ref, pair), hides[...]], axis=1)
        peak = None
        for b in range(KEYS // KEY_BLOCK):
            rows = slice(b * KEY_BLOCK, (b + 1) * KEY_BLOCK)
            block = dot_nt(masked_keys[g, rows, :], queries)
            scores[rows, :] = block
            top = jnp.max(block, axis=0, keepdims=True)
            peak = top if peak is None else jnp.maximum(peak, top)
        total, out = None, None
        for b in range(KEYS // KEY_BLOCK):
            rows = slice(b * KEY_BLOCK, (b + 1) * KEY_BLOCK)
            exps = jnp.exp2((scores[rows, :] - peak) * TO_BASE_TWO)
            part = jnp.sum(exps, axis=0, keepdims=True)
            piece = dot_nn(values_t[g, :, rows], exps.astype(BF))
            total = part if total is None else total + part
            out = piece if out is None else out + piece
        put_two_heads(mixed_ref, pair, (out / total).T.astype(BF))
        spread_ref[pl.ds(pair, 1), :] = peak * TO_BASE_TWO + jnp.log2(total)
        return carry

    lax.fori_loop(0, PAIRS, step, 0)
    features = mixed_ref[...].astype(F32)
    normed = (features * rms_factor(features) * gain_ref[...]).astype(BF)
    masks, _ = slot_masks(ids_ref, gates_ref, trainable_ref)
    picked = dot_nn(masks[0], fold_of(normed, 0))
    for f in range(1, FOLDS):
        picked = picked + dot_nn(masks[f], fold_of(normed, f))
    slab_ref[...] = picked.astype(BF)


def expert_kernel(rows_ref, grads_ref, w_ref, terms_ref, back_ref, routed, weighted, returned):
    step = pl.program_id(0)

    @pl.when(step == 0)
    def _():
        for f in range(FOLDS):
            pick = unfold_mask(f)
            routed[:, f * WIDE : (f + 1) * WIDE] = dot_nn(pick, rows_ref[...]).astype(BF)
            weighted[:, f * WIDE : (f + 1) * WIDE] = dot_nn(pick, grads_ref[...]).astype(BF)

    gate_in = dot_nt(routed[...], w_ref[0])
    up_in = dot_nt(routed[...], w_ref[1])
    back = dot_nt(weighted[...], w_ref[2])
    sigma = jax.nn.sigmoid(gate_in)
    activated = gate_in * sigma
    grad_gate = (back * up_in * sigma * (1.0 + gate_in * (1.0 - sigma))).astype(BF)
    grad_up = (back * activated).astype(BF)
    terms_ref[0] = grad_gate
    terms_ref[1] = grad_up
    terms_ref[2] = (activated * up_in).astype(BF)
    for f in range(FOLDS):
        at = slice(f * WIDE, (f + 1) * WIDE)
        part = dot_nn(grad_gate, w_ref[0, :, at]) + dot_nn(grad_up, w_ref[1, :, at])

        @pl.when(step == 0)
        def _():
            returned[:, at] = part

        @pl.when(step > 0)
        def _():
            returned[:, at] += part

    @pl.when(step == pl.num_programs(0) - 1)
    def _():
        total = dot_nn(refold_mask(0), returned[:, :WIDE].astype(BF))
        for f in range(1, FOLDS):
            at = slice(f * WIDE, (f + 1) * WIDE)
            total = total + dot_nn(refold_mask(f), returned[:, at].astype(BF))
        back_ref[...] = total.astype(BF)


def terms_kernel(own_ref, other_ref, own_terms_ref, other_terms_ref, out_ref):
    for f in range(FOLDS):
        pick = unfold_mask(f)
        own = dot_nn(pick, own_ref[...]).astype(BF)
        other = dot_nn(pick, other_ref[...]).astype(BF)
        for i in range(out_ref.shape[0]):
            out_ref[i, :, f * WIDE : (f + 1) * WIDE] = (
                dot_tn(own_terms_ref[i], own) + dot_tn(other_terms_ref[i], other)
            ).astype(BF)


def backward_kernel(
    q_ref, kv_ref, hidden_ref, ids_ref, gates_ref, trainable_ref, gain_ref,
    mixed_ref, spread_ref, up_ref, echo_ref,
    d_query_ref, d_kv_ref,
    masked_keys, keys_t, hides, grad_mixed, key_sums, value_sums,
):
    for g in range(KEY_VALUE_HEADS):
        keys = kv_ref[:, g * HEAD_SIZE : (g + 1) * HEAD_SIZE]
        masked_keys[g, :, :HEAD_SIZE] = keys
        masked_keys[g, :, HEAD_SIZE:] = hidden_ref[...]
        keys_t[g] = keys.T
    hides[...] = diagonal()
    key_sums[...] = jnp.zeros_like(key_sums)
    value_sums[...] = jnp.zeros_like(value_sums)

    masks, _ = slot_masks(ids_ref, gates_ref, trainable_ref)
    features = mixed_ref[...].astype(F32)
    factor = rms_factor(features)
    gradnorm = gain_ref[...] * jnp.concatenate(
        [dot_tn(m, echo_ref[...]) for m in masks], axis=1
    )
    across = jnp.mean(gradnorm * features, axis=1, keepdims=True)
    grad_mixed[...] = (
        up_ref[...].astype(F32)
        + factor * gradnorm
        - features * (factor * factor * factor) * across
    ).astype(BF)

    def step(pair, carry):
        g = lax.div(pair, PAIRS // KEY_VALUE_HEADS)
        plain = two_heads(q_ref, pair)
        queries = jnp.concatenate([plain, hides[...]], axis=1)
        grads = two_heads(grad_mixed, pair)
        products = grads.astype(F32) * two_heads(mixed_ref, pair).astype(F32)
        delta = jnp.sum(products.T, axis=0, keepdims=True)
        spread = spread_ref[pl.ds(pair, 1), :]
        d_query = None
        for b in range(KEYS // KEY_BLOCK):
            rows = slice(b * KEY_BLOCK, (b + 1) * KEY_BLOCK)
            at = (KEY_VALUE_HEADS + g) * HEAD_SIZE
            values = kv_ref[rows, pl.ds(pl.multiple_of(at, HEAD_SIZE), HEAD_SIZE)]
            raw = dot_nt(masked_keys[g, rows, :], queries)
            probs = jnp.exp2(raw * TO_BASE_TWO - spread)
            pushed = dot_nt(values, grads)
            slopes = (probs * (pushed - delta)).astype(BF)
            value_sums[g, rows, :] += dot_nn(probs.astype(BF), grads)
            key_sums[g, rows, :] += dot_nn(slopes, plain)
            piece = dot_nn(keys_t[g, :, rows], slopes)
            d_query = piece if d_query is None else d_query + piece
        put_two_heads(d_query_ref, pair, (d_query * INV_ROOT).T.astype(BF))
        return carry

    lax.fori_loop(0, PAIRS, step, 0)
    for g in range(KEY_VALUE_HEADS):
        at = g * HEAD_SIZE
        d_kv_ref[:, at : at + HEAD_SIZE] = (key_sums[g] * INV_ROOT).astype(BF)
        at = (KEY_VALUE_HEADS + g) * HEAD_SIZE
        d_kv_ref[:, at : at + HEAD_SIZE] = value_sums[g].astype(BF)


def greet(targets):
    barrier = pltpu.get_barrier_semaphore()
    for target in targets:
        pl.semaphore_signal(barrier, inc=1, device_id={"ctx": target}, device_id_type=MESH)
    pl.semaphore_wait(barrier, len(targets))


def send(source, target, send_sem, recv_sem, device):
    return pltpu.make_async_remote_copy(
        src_ref=source, dst_ref=target, send_sem=send_sem, recv_sem=recv_sem,
        device_id={"ctx": device}, device_id_type=MESH,
    )


def exchange_kernel(x_ref, out_ref, send_sem, recv_sem, own_sem):
    me = lax.axis_index("ctx")
    others = [lax.rem(me + d, N_CTX) for d in range(1, N_CTX)]
    greet(others)
    copies = []
    for d, other in enumerate(others):
        copy = send(x_ref.at[other], out_ref.at[me], send_sem.at[d], recv_sem.at[d], other)
        copy.start()
        copies.append(copy)
    own = pltpu.make_async_copy(x_ref.at[me], out_ref.at[me], own_sem)
    own.start()
    for copy in copies:
        copy.wait()
    own.wait()


def gather_kernel(x_ref, out_ref, send_sem, recv_sem, pass_sem, passed_sem, near_sem, own_sem):
    me = lax.axis_index("ctx")
    chip, core = lax.div(me, 2), lax.rem(me, 2)
    sibling = 2 * chip + 1 - core
    far = [2 * lax.rem(chip + d, N_CHIP) + core for d in range(1, N_CHIP)]
    greet([*far, sibling])
    copies = []
    for d, other in enumerate(far):
        copy = send(x_ref, out_ref.at[me], send_sem.at[d], recv_sem.at[d], other)
        copy.start()
        copies.append(copy)
    near = send(x_ref, out_ref.at[me], near_sem.at[0], near_sem.at[1], sibling)
    near.start()
    own = pltpu.make_async_copy(x_ref, out_ref.at[me], own_sem)
    own.start()
    passed = []
    for d in range(1, N_CHIP):
        source = 2 * lax.rem(chip + N_CHIP - d, N_CHIP) + core
        copies[d - 1].wait_recv()
        copy = send(
            out_ref.at[source], out_ref.at[source],
            pass_sem.at[d - 1], passed_sem.at[d - 1], sibling,
        )
        copy.start()
        passed.append(copy)
    for copy in copies:
        copy.wait_send()
    near.wait()
    own.wait()
    for copy in passed:
        copy.wait()


def scatter_kernel(
    x_ref, out_ref, near, sums, landed, near_send, near_recv, send_sem, recv_sem
):
    me = lax.axis_index("ctx")
    chip, core = lax.div(me, 2), lax.rem(me, 2)
    sibling = 2 * chip + 1 - core
    chips = [lax.rem(chip + d, N_CHIP) for d in range(N_CHIP)]
    greet([*(2 * c + core for c in chips[1:]), sibling])
    order = [*range(1, N_CHIP), 0]
    shared = {}
    for d in order:
        copy = send(
            x_ref.at[2 * chips[d] + 1 - core], near.at[d], near_send.at[d], near_recv.at[d], sibling
        )
        copy.start()
        shared[d] = copy
    copies = []
    for d in order:
        shared[d].wait_recv()
        both = x_ref[2 * chips[d] + core].astype(F32) + near[d].astype(F32)
        if d == 0:
            total = both
        else:
            sums[d] = both.astype(BF)
            copy = send(
                sums.at[d], landed.at[d], send_sem.at[d], recv_sem.at[d], 2 * chips[d] + core
            )
            copy.start()
            copies.append(copy)
    for d, copy in enumerate(copies, start=1):
        copy.wait_recv()
        total = total + landed[d].astype(F32)
    out_ref[...] = total.astype(BF)
    for copy in copies:
        copy.wait_send()
    for d in order:
        shared[d].wait_send()


def dma(count):
    return pltpu.SemaphoreType.DMA((count,))


def remote(kernel, shape, scratch, number, sent):
    return pl.pallas_call(
        kernel,
        out_shape=jax.ShapeDtypeStruct(shape, BF),
        in_specs=in_vmem(1),
        out_specs=in_vmem(1)[0],
        scratch_shapes=scratch,
        compiler_params=pltpu.CompilerParams(
            collective_id=number, has_side_effects=True, vmem_limit_bytes=VMEM_LIMIT
        ),
        cost_estimate=pl.CostEstimate(flops=0, bytes_accessed=sent, transcendentals=0),
    )


def exchange(slabs, number):
    shape = (SLOTS, SLAB, WIDE)
    scratch = [dma(N_CTX - 1), dma(N_CTX - 1), pltpu.SemaphoreType.DMA]
    out = remote(exchange_kernel, shape, scratch, number, 2**26)(slabs.reshape(shape))
    return out.reshape(SLAB_ROWS, WIDE)


def gather(block):
    scratch = [dma(7), dma(7), dma(7), dma(7), dma(2), pltpu.SemaphoreType.DMA]
    out = remote(gather_kernel, (N_CTX, *block.shape), scratch, 0, 2**26)(block)
    return out.reshape(-1, block.shape[1])


def scatter_sum(parts):
    blocks = parts.reshape(N_CTX, ROWS, -1)
    block = blocks.shape[1:]
    slots = pltpu.VMEM((N_CHIP, *block), BF)
    scratch = [slots, slots, slots, dma(8), dma(8), dma(8), dma(8)]
    return remote(scatter_kernel, block, scratch, 3, 2**26)(blocks)


def over_pair(array):
    return lax.ppermute(array, "dp", [(i, (i + 4) % 8) for i in range(8)])


def summed_over_x(array):
    return lax.psum_scatter(
        array, "dp", scatter_dimension=1, tiled=True,
        axis_index_groups=[[0, 1, 2, 3], [4, 5, 6, 7]],
    )


def per_device(
    query, key, value, span_order, expert_ids, expert_gates,
    trainable, norm_gain, upstream, expert_weights,
):
    bf_shape = lambda *s: jax.ShapeDtypeStruct(s, BF)
    half = ROWS // 2
    place = (span_order[0][:, None] * half + jnp.arange(half, dtype=jnp.int32)[None, :]).reshape(-1)
    own_place = lax.dynamic_slice_in_dim(place, lax.axis_index("ctx") * ROWS, ROWS)
    hidden = (place[:, None] > own_place[None, :]).astype(BF)
    tables = (expert_ids[0].T, expert_gates[0].T, trainable[:, None])
    gain = norm_gain[None, :]
    weights = expert_weights[0].transpose(1, 0, 2)

    slab_shape = bf_shape(SLAB_ROWS, WIDE)
    sent_grads = pl.pallas_call(
        weighted_kernel, out_shape=slab_shape, in_specs=in_vmem(4), out_specs=in_vmem(1)[0],
        name="weighted", **local(10**9),
    )(*tables, upstream[0])
    grads = lax.all_to_all(
        sent_grads.reshape(SLOTS, SLAB, WIDE), "ctx", split_axis=0, concat_axis=0, tiled=True
    ).reshape(SLAB_ROWS, WIDE)
    other_grads = over_pair(grads)

    whole = gather(jnp.concatenate([key[0], value[0]], axis=1))
    groups = KEY_VALUE_HEADS
    mixed, spread, sent_rows = pl.pallas_call(
        forward_kernel,
        out_shape=(
            bf_shape(ROWS, D),
            jax.ShapeDtypeStruct((PAIRS, 2 * ROWS), F32),
            slab_shape,
        ),
        in_specs=in_vmem(7),
        out_specs=tuple(in_vmem(3)),
        scratch_shapes=[
            pltpu.VMEM((groups, KEYS, 2 * HEAD_SIZE), BF),
            pltpu.VMEM((groups, HEAD_SIZE, KEYS), BF),
            pltpu.VMEM((2 * ROWS, ROWS), BF),
            pltpu.VMEM((KEYS, 2 * ROWS), F32),
        ],
        name="attention",
        **local(2 * 10**10),
    )(query[0], whole, hidden, *tables, gain)

    rows = exchange(sent_rows, 1)
    other_rows = over_pair(rows)

    block = 256
    terms, sent_back = pl.pallas_call(
        expert_kernel,
        grid=(H // block,),
        out_shape=(bf_shape(3, SLOTS * CAP, H), slab_shape),
        in_specs=[
            pl.BlockSpec((SLAB_ROWS, WIDE), lambda i: (0, 0)),
            pl.BlockSpec((SLAB_ROWS, WIDE), lambda i: (0, 0)),
            pl.BlockSpec((3, block, D), lambda i: (0, i, 0)),
        ],
        out_specs=(
            pl.BlockSpec((3, SLOTS * CAP, block), lambda i: (0, 0, i)),
            pl.BlockSpec((SLAB_ROWS, WIDE), lambda i: (0, 0)),
        ),
        scratch_shapes=[
            pltpu.VMEM((SLOTS * CAP, D), BF),
            pltpu.VMEM((SLOTS * CAP, D), BF),
            pltpu.VMEM((SLOTS * CAP, D), F32),
        ],
        name="experts",
        **local(10**10),
    )(rows, grads, weights)

    mine = lax.div(lax.axis_index("dp"), 4)
    kept = lax.dynamic_slice_in_dim(terms, mine * (H // 2), H // 2, 2)
    given = lax.dynamic_slice_in_dim(terms, (1 - mine) * (H // 2), H // 2, 2)
    taken = over_pair(given)

    def partial(own, other, at, count, name):
        return pl.pallas_call(
            terms_kernel, out_shape=bf_shape(count, H // 2, D),
            in_specs=in_vmem(4), out_specs=in_vmem(1)[0], name=name, **local(4 * 10**9),
        )(own, other, kept[at : at + count], taken[at : at + count])

    down = summed_over_x(partial(grads, other_grads, 2, 1, "down_terms"))
    echo = exchange(sent_back, 2)
    gate_up = summed_over_x(partial(rows, other_rows, 0, 2, "gate_up_terms"))

    d_query, d_kv = pl.pallas_call(
        backward_kernel,
        out_shape=(bf_shape(ROWS, D), bf_shape(KEYS, 2 * groups * HEAD_SIZE)),
        in_specs=in_vmem(11),
        out_specs=tuple(in_vmem(2)),
        scratch_shapes=[
            pltpu.VMEM((groups, KEYS, 2 * HEAD_SIZE), BF),
            pltpu.VMEM((groups, HEAD_SIZE, KEYS), BF),
            pltpu.VMEM((2 * ROWS, ROWS), BF),
            pltpu.VMEM((ROWS, D), BF),
            pltpu.VMEM((groups, KEYS, HEAD_SIZE), F32),
            pltpu.VMEM((groups, KEYS, HEAD_SIZE), F32),
        ],
        name="attention_grads",
        **local(4 * 10**10),
    )(query[0], whole, hidden, *tables, gain, mixed, spread, upstream[0], echo)
    kv_sums = scatter_sum(d_kv)
    split = groups * HEAD_SIZE
    expert_grads = jnp.concatenate([gate_up, down], axis=0).transpose(1, 0, 2)
    return (
        d_query[None],
        kv_sums[None, :, :split],
        kv_sums[None, :, split:],
        expert_grads[None],
    )


def solution(mesh):
    in_specs = (
        P("dp", "ctx", None),
        P("dp", "ctx", None),
        P("dp", "ctx", None),
        P("dp", None),
        P("dp", "ctx", None),
        P("dp", "ctx", None),
        P(),
        P(),
        P("dp", "ctx", None),
        P("ctx", None, None, None),
    )
    out_specs = (
        P("dp", "ctx", None),
        P("dp", "ctx", None),
        P("dp", "ctx", None),
        P("ctx", "dp", None, None),
    )
    return jax.shard_map(
        per_device, mesh=mesh, in_specs=in_specs, out_specs=out_specs, check_vma=False
    )
```

profile of v0, /device:TPU:1, one launch (start us, length us, event | category | flops | bytes accessed | tf_op | source)
XLA Modules:
  0.0 300.4 jit_solution(4029209325022122722)
XLA Ops:
  7.2 1.3 copy.16.trainable_ref
  8.5 4.4 %weighted.1 = bf16[768,1024]{1,0:T(8,128)(2,1)} custom-call(s32[8,128]{1,0:T(8,128)} %bitcast.57, f32[8,128]{1,0:T(8,128)} %bitcast.60, s32[16,1]{1,0:T(8,128)} %copy.16.trainable_ref, bf16[128,4096]{1,0:T(8,128)(2,1)} %bitcast.53), custom_call_target="tpu_custom_call" | custom-call | flops 1000000000 | bytes 4194304 | tf_op jit(solution)/shard_map/weighted/pallas_call | solution.py:465
  12.9 8.0 %all-to-all-start = ((bf16[16,48,1024]{2,1,0:T(8,128)(2,1)}), bf16[16,48,1024]{2,1,0:T(8,128)(2,1)S(1)}, u32[]{:S(2)}, u32[]{:S(2)}) async-start(bf16[16,48,1024]{2,1,0:T(8,128)(2,1)} %bitcast.44), calls=%async_computation | async-start | bytes 3145728 | tf_op jit(solution)/shard_map/all_to_all | solution.py:469
  20.9 0.0 reduce-scatter.5.cloned.1.call-start
  21.0 0.7 pad_maximum_fusion.x_ref
  21.6 35.1 %shard_map.129 = bf16[16,128,512]{2,1,0:T(8,128)(2,1)} custom-call(bf16[128,512]{1,0:T(8,128)(2,1)} %pad_maximum_fusion.x_ref), custom_call_target="tpu_custom_call" | custom-call | bytes 67108864 | tf_op jit(solution)/shard_map/pallas_call | solution.py:428
  56.7 0.1 iota_add_fusion
  56.8 0.1 add.37
  56.9 0.1 dynamic_slice.9
  56.9 1.1 compare_convert_fusion.hidden_ref
  58.1 2.6 collective-permute-start.2
  60.7 27.7 %attention.1 = (bf16[128,4096]{1,0:T(8,128)(2,1)}, f32[16,256]{1,0:T(8,128)}, bf16[768,1024]{1,0:T(8,128)(2,1)}) custom-call(bf16[128,4096]{1,0:T(8,128)(2,1)} %bitcast.51, bf16[2048,512]{1,0:T(8,128)(2,1)} %bitcast.34, bf16[2048,128]{1,0:T(8,128)(2,1)} %compare_convert_fusion.hidden_ref, s32[8,128]{1,0:T(8,128)} %bitcast.58, f32[8,128]{1,0:T(8,128)} %bitcast.61, ...), custom_call_target="tpu_custom_call" | custom-call | flops 20000000000 | bytes 4194304 | tf_op jit(solution)/shard_map/attention/pallas_call | solution.py:476
  88.4 26.4 %shard_map.130 = bf16[16,48,1024]{2,1,0:T(8,128)(2,1)} custom-call(bf16[16,48,1024]{2,1,0:T(8,128)(2,1)} %bitcast.45), custom_call_target="tpu_custom_call" | custom-call | bytes 67108864 | tf_op jit(solution)/shard_map/pallas_call | solution.py:422
  114.9 24.1 %experts.1 = (bf16[3,192,768]{2,1,0:T(8,128)(2,1)}, bf16[768,1024]{1,0:T(8,128)(2,1)}) custom-call(bf16[768,1024]{1,0:T(8,128)(2,1)} %bitcast.40, bf16[768,1024]{1,0:T(8,128)(2,1)} %bitcast.38, bf16[3,768,4096]{2,1,0:T(8,128)(2,1)} %bitcast.50), custom_call_target="tpu_custom_call" | custom-call | flops 10000000000 | bytes 4194304 | tf_op jit(solution)/shard_map/experts/pallas_call | solution.py:499
  139.0 1.1 constant_dynamic-slice_fusion.1
  140.1 1.9 collective-permute-start.1
  141.9 1.6 constant_dynamic-slice_fusion.2.own_terms_ref
  143.5 10.3 %collective-permute-done.1 = bf16[3,192,384]{2,1,0:T(8,128)(2,1)S(1)} collective-permute-done((bf16[3,192,384]{2,1,0:T(8,128)(2,1)S(1)}, bf16[3,192,384]{2,1,0:T(8,128)(2,1)S(1)}, u32[]{:S(2)}, u32[]{:S(2)}) %collective-permute-start.1) | collective-permute-done | bytes 442400 | tf_op jit(solution)/shard_map/ppermute | solution.py:441
  153.8 0.7 slice.25.other_terms_ref
  154.5 8.0 %down_terms.1 = bf16[1,384,4096]{2,1,0:T(8,128)(2,1)} custom-call(bf16[768,1024]{1,0:T(8,128)(2,1)} %bitcast.39, bf16[768,1024]{1,0:T(8,128)(2,1)} %collective-permute-done.2.other_ref, bf16[1,192,384]{2,1,0:T(8,128)(2,1)} %constant_dynamic-slice_fusion.2.own_terms_ref, bf16[1,192,384]{2,1,0:T(8,128)(2,1)} %slice.25.other_terms_ref), custom_call_target="tpu_custom_call" | custom-call | flops 4000000000 | bytes 4194304 | tf_op jit(solution)/shard_map/down_terms/pallas_call | solution.py:527
  162.5 0.0 reduce-scatter.3.cloned.1.call-start
  162.6 1.3 copy-done.1
  163.9 1.1 collective-permute-start
  165.0 1.7 constant_dynamic-slice_fusion.own_terms_ref
  166.7 0.7 slice.24.other_terms_ref
  167.4 33.7 %collective-permute-done.other_ref = bf16[768,1024]{1,0:T(8,128)(2,1)} collective-permute-done((bf16[768,1024]{1,0:T(8,128)(2,1)S(1)}, bf16[768,1024]{1,0:T(8,128)(2,1)}, u32[]{:S(2)}, u32[]{:S(2)}) %collective-permute-start) | collective-permute-done | bytes 1572896 | tf_op jit(solution)/shard_map/ppermute | solution.py:441
  201.1 10.6 %gate_up_terms.1 = bf16[2,384,4096]{2,1,0:T(8,128)(2,1)} custom-call(bf16[768,1024]{1,0:T(8,128)(2,1)} %bitcast.41, bf16[768,1024]{1,0:T(8,128)(2,1)} %collective-permute-done.other_ref, bf16[2,192,384]{2,1,0:T(8,128)(2,1)} %constant_dynamic-slice_fusion.own_terms_ref, bf16[2,192,384]{2,1,0:T(8,128)(2,1)} %slice.24.other_terms_ref), custom_call_target="tpu_custom_call" | custom-call | flops 4000000000 | bytes 4194304 | tf_op jit(solution)/shard_map/gate_up_terms/pallas_call | solution.py:527
  211.8 25.8 %shard_map.131 = bf16[16,48,1024]{2,1,0:T(8,128)(2,1)} custom-call(bf16[16,48,1024]{2,1,0:T(8,128)(2,1)} %bitcast.43), custom_call_target="tpu_custom_call" | custom-call | bytes 67108864 | tf_op jit(solution)/shard_map/pallas_call | solution.py:422
  237.5 31.8 %attention_grads.1 = (bf16[128,4096]{1,0:T(8,128)(2,1)}, bf16[2048,512]{1,0:T(8,128)(2,1)}) custom-call(bf16[128,4096]{1,0:T(8,128)(2,1)} %bitcast.52, bf16[2048,512]{1,0:T(8,128)(2,1)} %bitcast.35, bf16[2048,128]{1,0:T(8,128)(2,1)} %compare_convert_fusion.hidden_ref, s32[8,128]{1,0:T(8,128)} %bitcast.59, f32[8,128]{1,0:T(8,128)} %bitcast.62, ...), custom_call_target="tpu_custom_call" | custom-call | flops 40000000000 | bytes 4194304 | tf_op jit(solution)/shard_map/attention_grads/pallas_call | solution.py:536
  269.3 19.5 %shard_map.132 = bf16[128,512]{1,0:T(8,128)(2,1)} custom-call(bf16[16,128,512]{2,1,0:T(8,128)(2,1)} %bitcast.36), custom_call_target="tpu_custom_call" | custom-call | bytes 67108864 | tf_op jit(solution)/shard_map/pallas_call | solution.py:437
  288.8 1.5 slice_bitcast_fusion
  290.3 3.3 %maximum_bitcast_fusion = bf16[1,96,3,4096]{3,1,2,0:T(8,128)(2,1)} fusion(bf16[1,96,4096]{2,1,0:T(8,128)(2,1)} %reduce-scatter.5.cloned.1.call-done, bf16[2,96,4096]{2,1,0:T(8,128)(2,1)} %reduce-scatter.3.cloned.1.call-done), kind=kLoop, calls=%fused_computation | loop fusion | flops 1179648 | bytes 4718592 | tf_op jit(solution)/shard_map/broadcast_in_dim | solution.py:559
  (16 shorter events, 0.1 us)
Async XLA Ops:
  12.9 8.0 %copy-start.2 = (bf16[1,128,256]{2,1,0:T(8,128)(2,1)S(1)}, bf16[1,128,256]{2,1,0:T(8,128)(2,1)}, u32[]{:S(2)}) copy-start(bf16[1,128,256]{2,1,0:T(8,128)(2,1)} %param.12) | copy-start | bytes 196612
  12.9 8.1 %copy-start.3 = (bf16[1,128,256]{2,1,0:T(8,128)(2,1)S(1)}, bf16[1,128,256]{2,1,0:T(8,128)(2,1)}, u32[]{:S(2)}) copy-start(bf16[1,128,256]{2,1,0:T(8,128)(2,1)} %param.11) | copy-start | bytes 196612
  12.9 45.2 %all-to-all-start = ((bf16[16,48,1024]{2,1,0:T(8,128)(2,1)}), bf16[16,48,1024]{2,1,0:T(8,128)(2,1)S(1)}, u32[]{:S(2)}, u32[]{:S(2)}) async-start(bf16[16,48,1024]{2,1,0:T(8,128)(2,1)} %bitcast.44), calls=%async_computation | async-start | bytes 3145728 | tf_op jit(solution)/shard_map/all_to_all | solution.py:469
  20.9 35.8 %copy-start.4 = (s32[1,32]{1,0:T(1,128)S(1)}, s32[1,32]{1,0:T(1,128)}, u32[]{:S(2)}) copy-start(s32[1,32]{1,0:T(1,128)} %param.13) | copy-start | bytes 388
  20.9 269.4 %reduce-scatter.5.cloned.1.call-start = ((), (), s32[]{:S(2)}) async-start(), calls=%async_computation.4 | async-start | bytes 3932160 | tf_op jit(solution)/shard_map/reduce_scatter | solution.py:445
  58.1 30.4 %copy-start = (bf16[16,48,1024]{2,1,0:T(8,128)(2,1)}, bf16[16,48,1024]{2,1,0:T(8,128)(2,1)S(1)}, u32[]{:S(2)}) copy-start(bf16[16,48,1024]{2,1,0:T(8,128)(2,1)S(1)} %all-to-all-done) | copy-start | bytes 4718596
  58.1 96.4 %collective-permute-start.2 = (bf16[768,1024]{1,0:T(8,128)(2,1)S(1)}, bf16[768,1024]{1,0:T(8,128)(2,1)}, u32[]{:S(2)}, u32[]{:S(2)}) collective-permute-start(bf16[768,1024]{1,0:T(8,128)(2,1)S(1)} %bitcast.37), channel_id=1, source_target_pairs={{0,64},{16,80},{32,96},{48,112},{64,0},{80,16},{96,32},{112,48},{1... | collective-permute-start | bytes 4718600 | tf_op jit(solution)/shard_map/ppermute | solution.py:441
  140.1 13.8 %collective-permute-start.1 = (bf16[3,192,384]{2,1,0:T(8,128)(2,1)S(1)}, bf16[3,192,384]{2,1,0:T(8,128)(2,1)S(1)}, u32[]{:S(2)}, u32[]{:S(2)}) collective-permute-start(bf16[3,192,384]{2,1,0:T(8,128)(2,1)S(1)} %constant_dynamic-slice_fusion.1), channel_id=1, source_target_pairs={{0,64},{16,80},{32,96},{48,112},{64,0},{80,16},{96,32},{112,48},{1... | collective-permute-start | bytes 1327112 | tf_op jit(solution)/shard_map/ppermute | solution.py:441
  162.5 1.4 copy-start.1
  162.5 127.8 %reduce-scatter.3.cloned.1.call-start = ((), (), s32[]{:S(2)}) async-start(), calls=%async_computation.3 | async-start | bytes 7864320 | tf_op jit(solution)/shard_map/reduce_scatter | solution.py:445
  163.9 37.2 %collective-permute-start = (bf16[768,1024]{1,0:T(8,128)(2,1)S(1)}, bf16[768,1024]{1,0:T(8,128)(2,1)}, u32[]{:S(2)}, u32[]{:S(2)}) collective-permute-start(bf16[768,1024]{1,0:T(8,128)(2,1)S(1)} %bitcast.42), channel_id=1, source_target_pairs={{0,64},{16,80},{32,96},{48,112},{64,0},{80,16},{96,32},{112,48},{1... | collective-permute-start | bytes 4718600 | tf_op jit(solution)/shard_map/ppermute | solution.py:441
Sparse Core Ops, SparseCore 0:
  162.6 36.6 reduce-scatter.4
  211.9 63.1 reduce-scatter.2
where the time goes:
time: 301 us; the launch traced here: 300 us
  Pallas kernels  213 us (71%)
  waiting for transfers between devices  44 us (15%)
  between operations  14.1 us (5%)
  starting transfers between devices  13.6 us (5%)
  local copies, waits for them, and re-layouts  10.1 us (3%)
  other arithmetic  5.14 us (2%)
    pallas_call x2, Pallas kernels, exchange(): remote(exchange_kernel, shape, scratch, number, 2 ** 26)  52.2 us
    ppermute x3, waiting for transfers between devices, over_pair(): return lax.ppermute(array, 'dp', [(i, (i + 4) % 8) for i in range(8)])  44 us
    pallas_call x1, Pallas kernels, gather(): remote(gather_kernel, (N_CTX, *block.shape), scratch, 0, 2 ** 26)(block)  35.1 us
    pallas_call x1, Pallas kernels, per_device(): pl.pallas_call(backward_kernel, out_shape=(bf_shape(ROWS, D), bf_shape(KE...  31.8 us
    pallas_call x1, Pallas kernels, per_device(): pl.pallas_call(forward_kernel, out_shape=(bf_shape(ROWS, D), jax.ShapeDty...  27.7 us
    pallas_call x1, Pallas kernels, per_device(): pl.pallas_call(expert_kernel, grid=(H // block,), out_shape=(bf_shape(3,...  24.1 us
    pallas_call x1, Pallas kernels, scatter_sum(): return remote(scatter_kernel, block, scratch, 3, 2 ** 26)(blocks)  19.5 us
    pallas_call x2, Pallas kernels, partial(): pl.pallas_call(terms_kernel, out_shape=bf_shape(count, H // 2, D), in_spe...  18.6 us
  transfers between devices with their start and end apart: 6, of which 2 were waited for; matrix products, arithmetic and copies ran while one was open for 3% of the time, Pallas kernels for 67%

commit v1 on v0

v1 whole, which is shorter than its diff:
```python
import math

import jax
import jax.numpy as jnp
from jax import lax
from jax.experimental import pallas as pl
from jax.experimental.pallas import tpu as pltpu
from jax.sharding import PartitionSpec as P

D = 4096
QUERY_HEADS = 32
KEY_VALUE_HEADS = 2
HEAD_SIZE = 128
TOP = 8
CAP = 12
H = 768
N_CTX = 16
N_CHIP = 8
ROWS = 128
KEYS = 2048
SLOTS = 16
FOLDS = 4
WIDE = D // FOLDS
SLAB = CAP * FOLDS
SLAB_ROWS = SLOTS * SLAB
PAIRS = QUERY_HEADS // 2
KEY_BLOCK = 512
PART = H // 8

MASK_FILLER = -1e30
EPSILON = 1e-06
INV_ROOT = HEAD_SIZE ** (-0.5)
TO_BASE_TWO = INV_ROOT * math.log2(math.e)

X_GROUPS = [[0, 1, 2, 3], [4, 5, 6, 7]]
MESH = pl.DeviceIdType.MESH
VMEM_LIMIT = 60 * 2**20
BF = jnp.bfloat16
F32 = jnp.float32


def dot_nn(a, b):
    return lax.dot_general(a, b, (((1,), (0,)), ((), ())), preferred_element_type=F32)


def dot_nt(a, b):
    return lax.dot_general(a, b, (((1,), (1,)), ((), ())), preferred_element_type=F32)


def dot_tn(a, b):
    return lax.dot_general(a, b, (((0,), (0,)), ((), ())), preferred_element_type=F32)


def in_vmem(count):
    return [pl.BlockSpec(memory_space=pltpu.VMEM)] * count


def local(cost):
    return dict(
        compiler_params=pltpu.CompilerParams(vmem_limit_bytes=VMEM_LIMIT),
        cost_estimate=pl.CostEstimate(flops=cost, bytes_accessed=2**22, transcendentals=0),
    )


def expert_ranks(ids_ref, trainable_ref):
    hits = jnp.zeros((SLOTS, ROWS), F32)
    for k in range(TOP):
        hits = hits + jnp.where(ids_ref[k : k + 1, :] == trainable_ref[...], 1.0, 0.0)
    before = lax.broadcasted_iota(jnp.int32, (ROWS, ROWS), 0) < lax.broadcasted_iota(
        jnp.int32, (ROWS, ROWS), 1
    )
    rank = dot_nn(hits.astype(BF), jnp.where(before, 1.0, 0.0).astype(BF))
    return jnp.where(hits > 0.5, rank, -1.0)


def tenth(n):
    return lax.shift_right_logical(n * 5462, 16)


def slot_mask(rank, pad):
    rows = SLOTS * pad
    n = lax.broadcasted_iota(jnp.int32, (rows, SLOTS), 0)
    j = lax.broadcasted_iota(jnp.int32, (rows, SLOTS), 1)
    owner = tenth(n) if pad == CAP else lax.shift_right_logical(n, 4)
    spread = dot_nn(jnp.where(owner == j, 1.0, 0.0).astype(BF), rank.astype(BF))
    slot = n[:, :1] - pad * owner[:, :1]
    return spread == slot.astype(F32), owner


def swap_mask():
    o = lax.broadcasted_iota(jnp.int32, (4 * SLAB, 4 * SLAB), 0)
    i = lax.broadcasted_iota(jnp.int32, (4 * SLAB, 4 * SLAB), 1)
    a = sum(jnp.where(o >= SLAB * k, 1, 0) for k in range(1, 4))
    o = o - SLAB * a
    b = sum(jnp.where(o >= CAP * k, 1, 0) for k in range(1, 4))
    return jnp.where(i == SLAB * b + CAP * a + o - CAP * b, 1.0, 0.0).astype(BF)


def unfolded(slabs, swap):
    for g in range(4):
        rows = dot_nn(swap, slabs[g * 4 * SLAB : (g + 1) * 4 * SLAB])
        for a in range(FOLDS):
            yield slice(g * SLAB, (g + 1) * SLAB), a, rows[a * SLAB : (a + 1) * SLAB]


def folded(rows, swap):
    wide = rows.shape[1] // FOLDS
    slabs = []
    for g in range(4):
        at = slice(g * SLAB, (g + 1) * SLAB)
        pile = [rows[at, a * wide : (a + 1) * wide] for a in range(FOLDS)]
        slabs.append(dot_nn(swap, jnp.concatenate(pile, axis=0)).astype(BF))
    return jnp.concatenate(slabs, axis=0)


def exact(a, b):
    return lax.dot_general(
        a, b, (((1,), (0,)), ((), ())),
        precision=lax.Precision.HIGHEST, preferred_element_type=F32,
    )


def weighted_kernel(ids_ref, gates_ref, trainable_ref, up_ref, out_ref):
    rank = expert_ranks(ids_ref, trainable_ref)
    mask, owner = slot_mask(rank, CAP)
    gates = jnp.zeros((SLOTS, ROWS), F32)
    for k in range(TOP):
        same = ids_ref[k : k + 1, :] == trainable_ref[...]
        gates = gates + jnp.where(same, gates_ref[k : k + 1, :], 0.0)
    own = owner == lax.broadcasted_iota(jnp.int32, owner.shape, 1)
    gates = exact(jnp.where(own, 1.0, 0.0), gates)
    gate = jnp.sum(jnp.where(mask, gates, 0.0), axis=1, keepdims=True)
    rows = dot_nn(jnp.where(mask, 1.0, 0.0).astype(BF), up_ref[...])
    out_ref[...] = folded((gate * rows).astype(BF), swap_mask())


def two_heads(ref, pair):
    at = pl.multiple_of(pair * 2 * HEAD_SIZE, 2 * HEAD_SIZE)
    both = ref[:, pl.ds(at, 2 * HEAD_SIZE)]
    return jnp.concatenate([both[:, :HEAD_SIZE], both[:, HEAD_SIZE:]], axis=0)


def put_two_heads(ref, pair, stacked):
    at = pl.multiple_of(pair * 2 * HEAD_SIZE, 2 * HEAD_SIZE)
    ref[:, pl.ds(at, 2 * HEAD_SIZE)] = jnp.concatenate([stacked[:ROWS], stacked[ROWS:]], axis=1)


def diagonal():
    eye = lax.broadcasted_iota(jnp.int32, (ROWS, ROWS), 0) == lax.broadcasted_iota(
        jnp.int32, (ROWS, ROWS), 1
    )
    one = jnp.where(eye, MASK_FILLER, 0.0).astype(BF)
    return jnp.concatenate([one, one], axis=0)


def rms_factor(features):
    return lax.rsqrt(jnp.mean(features * features, axis=1, keepdims=True) + EPSILON)


def forward_kernel(
    kv_ref, slabs_ref, q_ref, hidden_ref, ids_ref, trainable_ref,
    whole_ref, slabs_out_ref, mixed_ref, spread_ref, rows_ref, factors_ref,
    masked_keys, values_t, hides, scores, sent_rows, sent_factors,
    send_sem, recv_sem, pass_sem, passed_sem, near_sem, own_sem,
    slab_send, slab_recv, row_send, row_recv, row_own, factor_send, factor_recv,
):
    me = lax.axis_index("ctx")
    chip, core = lax.div(me, 2), lax.rem(me, 2)
    sibling = 2 * chip + 1 - core
    far = [2 * lax.rem(chip + d, N_CHIP) + core for d in range(1, N_CHIP)]
    others = [lax.rem(me + d, N_CTX) for d in range(1, N_CTX)]
    greet(others)
    copies = []
    for d, other in enumerate(far):
        copy = send(kv_ref, whole_ref.at[me], send_sem.at[d], recv_sem.at[d], other)
        copy.start()
        copies.append(copy)
    near = send(kv_ref, whole_ref.at[me], near_sem.at[0], near_sem.at[1], sibling)
    near.start()
    own = pltpu.make_async_copy(kv_ref, whole_ref.at[me], own_sem.at[0])
    own.start()

    mask, _ = slot_mask(expert_ranks(ids_ref, trainable_ref), CAP)
    mask = jnp.where(mask, 1.0, 0.0).astype(BF)
    swap = swap_mask()
    hides[...] = diagonal()
    for g in range(KEY_VALUE_HEADS):
        masked_keys[g, :, HEAD_SIZE:] = hidden_ref[...]

    passed = []
    for d in range(1, N_CHIP):
        source = 2 * lax.rem(chip + N_CHIP - d, N_CHIP) + core
        copies[d - 1].wait_recv()
        copy = send(
            whole_ref.at[source], whole_ref.at[source],
            pass_sem.at[d - 1], passed_sem.at[d - 1], sibling,
        )
        copy.start()
        passed.append(copy)
    for copy in copies:
        copy.wait_send()
    near.wait()
    own.wait()
    for copy in passed:
        copy.wait()

    slabs = []
    for d, other in enumerate(others):
        copy = send(
            slabs_ref.at[other], slabs_out_ref.at[me], slab_send.at[d], slab_recv.at[d], other
        )
        copy.start()
        slabs.append(copy)
    own_slab = pltpu.make_async_copy(slabs_ref.at[me], slabs_out_ref.at[me], own_sem.at[1])
    own_slab.start()

    for g in range(KEY_VALUE_HEADS):
        at = g * HEAD_SIZE
        keys = whole_ref[:, :, at : at + HEAD_SIZE].reshape(KEYS, HEAD_SIZE)
        masked_keys[g, :, :HEAD_SIZE] = keys
        at = (KEY_VALUE_HEADS + g) * HEAD_SIZE
        values_t[g] = whole_ref[:, :, at : at + HEAD_SIZE].reshape(KEYS, HEAD_SIZE).T

    def step(pair, carry):
        g = lax.div(pair, PAIRS // KEY_VALUE_HEADS)
        queries = jnp.concatenate([two_heads(q_ref, pair), hides[...]], axis=1)
        peak = None
        for b in range(KEYS // KEY_BLOCK):
            rows = slice(b * KEY_BLOCK, (b + 1) * KEY_BLOCK)
            block = dot_nt(masked_keys[g, rows, :], queries)
            scores[rows, :] = block
            top = jnp.max(block, axis=0, keepdims=True)
            peak = top if peak is None else jnp.maximum(peak, top)
        total, out = None, None
        for b in range(KEYS // KEY_BLOCK):
            rows = slice(b * KEY_BLOCK, (b + 1) * KEY_BLOCK)
            exps = jnp.exp2((scores[rows, :] - peak) * TO_BASE_TWO)
            part = jnp.sum(exps, axis=0, keepdims=True)
            piece = dot_nn(values_t[g, :, rows], exps.astype(BF))
            total = part if total is None else total + part
            out = piece if out is None else out + piece
        put_two_heads(mixed_ref, pair, (out / total).T.astype(BF))
        spread_ref[pl.ds(pair, 1), :] = peak * TO_BASE_TWO + jnp.log2(total)
        return carry

    def row_copies(f):
        return [
            send(
                sent_rows.at[f, other], rows_ref.at[f, me],
                row_send.at[f, d], row_recv.at[f, d], other,
            )
            for d, other in enumerate(others)
        ]

    def own_rows(f):
        return pltpu.make_async_copy(sent_rows.at[f, me], rows_ref.at[f, me], row_own.at[f])

    def quarter(f, carry):
        lax.fori_loop(f * (PAIRS // FOLDS), (f + 1) * (PAIRS // FOLDS), step, 0)
        columns = mixed_ref[:, pl.ds(pl.multiple_of(f * WIDE, WIDE), WIDE)]
        picked = folded(dot_nn(mask, columns).astype(BF), swap)
        sent_rows[f] = picked.reshape(SLOTS, SLAB, WIDE // FOLDS)
        for copy in row_copies(f):
            copy.start()
        own_rows(f).start()
        return carry

    lax.fori_loop(0, FOLDS, quarter, 0)

    features = mixed_ref[...].astype(F32)
    factor = jnp.broadcast_to(rms_factor(features), (ROWS, 128))
    padded, _ = slot_mask(expert_ranks(ids_ref, trainable_ref), 16)
    picked = exact(jnp.where(padded, 1.0, 0.0), factor)
    sent_factors[...] = picked.reshape(SLOTS, 16, 128)
    factors = []
    for d, other in enumerate(others):
        copy = send(
            sent_factors.at[other], factors_ref.at[me], factor_send.at[d], factor_recv.at[d], other
        )
        copy.start()
        factors.append(copy)
    own_factor = pltpu.make_async_copy(sent_factors.at[me], factors_ref.at[me], own_sem.at[2])
    own_factor.start()

    for copy in slabs:
        copy.wait()
    own_slab.wait()

    def finish(f, carry):
        for copy in row_copies(f):
            copy.wait()
        own_rows(f).wait()
        return carry

    lax.fori_loop(0, FOLDS, finish, 0)
    for copy in factors:
        copy.wait()
    own_factor.wait()


def unfold_kernel(slab_ref, out_ref):
    for rows, a, values in unfolded(slab_ref[...], swap_mask()):
        out_ref[rows, a * WIDE : (a + 1) * WIDE] = values.astype(BF)


def norm_kernel(rows_ref, factors_ref, gain_ref, out_ref):
    n = lax.broadcasted_iota(jnp.int32, (SLOTS * CAP, SLOTS * 16), 0)
    m = lax.broadcasted_iota(jnp.int32, (SLOTS * CAP, SLOTS * 16), 1)
    kept = jnp.where(m == n + (16 - CAP) * tenth(n), 1.0, 0.0)
    factor = exact(kept, factors_ref[...])[:, :1]
    swap = swap_mask()
    narrow = WIDE // FOLDS
    for f in range(FOLDS):
        for rows, a, values in unfolded(rows_ref[f], swap):
            at = f * WIDE + a * narrow
            gain = gain_ref[:, at : at + narrow]
            out_ref[rows, at : at + narrow] = (values * factor[rows] * gain).astype(BF)


def expert_kernel(
    mine_ref, rows_ref, grads_ref, w_ref, terms_ref, products_ref, back_ref,
    routed_t, weighted_t, returned,
):
    step = pl.program_id(0)

    @pl.when(step == 0)
    def _():
        routed_t[...] = rows_ref[...].T
        weighted_t[...] = grads_ref[...].T

    gate_in = dot_nn(w_ref[0], routed_t[...])
    up_in = dot_nn(w_ref[1], routed_t[...])
    back = dot_nn(w_ref[2], weighted_t[...])
    sigma = jax.nn.sigmoid(gate_in)
    activated = gate_in * sigma
    grad_gate = (back * up_in * sigma * (1.0 + gate_in * (1.0 - sigma))).astype(BF)
    grad_up = (back * activated).astype(BF)
    place = lax.rem(step + mine_ref[0], 2)
    products_ref[place] = (activated * up_in).astype(BF)
    for x in range(4):
        terms_ref[x, place, 0] = grad_gate[x * PART : (x + 1) * PART]
        terms_ref[x, place, 1] = grad_up[x * PART : (x + 1) * PART]
    grad_gate, grad_up = grad_gate.T, grad_up.T
    for f in range(FOLDS):
        at = slice(f * WIDE, (f + 1) * WIDE)
        part = dot_nn(grad_gate, w_ref[0, :, at]) + dot_nn(grad_up, w_ref[1, :, at])

        @pl.when(step == 0)
        def _():
            returned[:, at] = part

        @pl.when(step > 0)
        def _():
            returned[:, at] += part

    @pl.when(step == pl.num_programs(0) - 1)
    def _():
        back_ref[...] = folded(returned[...].astype(BF), swap_mask())


def down_kernel(own_ref, other_ref, own_products_ref, other_products_ref, out_ref):
    out_ref[...] = (
        dot_nn(own_products_ref[...], own_ref[...])
        + dot_nn(other_products_ref[...], other_ref[...])
    ).astype(BF)


def gate_up_kernel(terms0, terms1, terms2, terms3, rows_ref, kept_ref, given_ref):
    x = lax.rem(lax.axis_index("dp"), 4)
    total = None
    for k, terms in enumerate((terms0, terms1, terms2, terms3)):
        left = terms[...].reshape(4 * PART, SLOTS * CAP)
        part = dot_nn(left, rows_ref[lax.rem(x + 4 - k, 4)])
        total = part if total is None else total + part
    kept_ref[...] = total[: 2 * PART].astype(BF)
    given_ref[...] = total[2 * PART :].astype(BF)


def fill_keys(kv_ref, hidden_ref, g, masked_keys, keys_t, hides):
    keys = kv_ref[:, g * HEAD_SIZE : (g + 1) * HEAD_SIZE]
    masked_keys[:, :HEAD_SIZE] = keys
    masked_keys[:, HEAD_SIZE:] = hidden_ref[...]
    keys_t[...] = keys.T
    hides[...] = diagonal()


def backward_pairs(
    g, q_ref, kv_ref, mixed_ref, spread_ref, grad_mixed_ref, d_query_ref,
    masked_keys, keys_t, hides, key_sums, value_sums,
):
    count = PAIRS // KEY_VALUE_HEADS
    skip = g * count - (d_query_ref.shape[1] // (2 * HEAD_SIZE) - count)
    key_sums[...] = jnp.zeros_like(key_sums)
    value_sums[...] = jnp.zeros_like(value_sums)
    at = (KEY_VALUE_HEADS + g) * HEAD_SIZE

    def step(pair, carry):
        plain = two_heads(q_ref, pair)
        queries = jnp.concatenate([plain, hides[...]], axis=1)
        grads = two_heads(grad_mixed_ref, pair)
        products = grads.astype(F32) * two_heads(mixed_ref, pair).astype(F32)
        delta = jnp.sum(products.T, axis=0, keepdims=True)
        spread = spread_ref[pl.ds(pair, 1), :]
        d_query = None
        for b in range(KEYS // KEY_BLOCK):
            rows = slice(b * KEY_BLOCK, (b + 1) * KEY_BLOCK)
            values = kv_ref[rows, at : at + HEAD_SIZE]
            raw = dot_nt(masked_keys[rows, :], queries)
            probs = jnp.exp2(raw * TO_BASE_TWO - spread)
            pushed = dot_nt(values, grads)
            slopes = (probs * (pushed - delta)).astype(BF)
            value_sums[rows, :] += dot_nn(probs.astype(BF), grads)
            key_sums[rows, :] += dot_nn(slopes, plain)
            piece = dot_nn(keys_t[:, rows], slopes)
            d_query = piece if d_query is None else d_query + piece
        put_two_heads(d_query_ref, pair - skip, (d_query * INV_ROOT).T.astype(BF))
        return carry

    lax.fori_loop(g * count, (g + 1) * count, step, 0)


def first_backward_kernel(
    q_ref, kv_ref, hidden_ref, ids_ref, trainable_ref, gain_ref,
    mixed_ref, spread_ref, up_ref, echo_ref,
    d_query_ref, d_kv_ref, grad_mixed_ref,
    masked_keys, keys_t, hides, key_sums, value_sums, echoed,
):
    mask, _ = slot_mask(expert_ranks(ids_ref, trainable_ref), CAP)
    mask = jnp.where(mask, 1.0, 0.0).astype(BF)
    for rows, a, values in unfolded(echo_ref[...], swap_mask()):
        echoed[rows, a * WIDE : (a + 1) * WIDE] = values.astype(BF)
    features = mixed_ref[...].astype(F32)
    factor = rms_factor(features)
    gradnorm = gain_ref[...] * dot_tn(mask, echoed[...])
    across = jnp.mean(gradnorm * features, axis=1, keepdims=True)
    grad_mixed_ref[...] = (
        up_ref[...].astype(F32)
        + factor * gradnorm
        - features * (factor * factor * factor) * across
    ).astype(BF)
    fill_keys(kv_ref, hidden_ref, 0, masked_keys, keys_t, hides)
    backward_pairs(
        0, q_ref, kv_ref, mixed_ref, spread_ref, grad_mixed_ref, d_query_ref,
        masked_keys, keys_t, hides, key_sums, value_sums,
    )
    d_kv_ref[:, :HEAD_SIZE] = (key_sums[...] * INV_ROOT).astype(BF)
    d_kv_ref[:, HEAD_SIZE:] = value_sums[...].astype(BF)


def second_backward_kernel(
    q_ref, kv_ref, hidden_ref, mixed_ref, spread_ref, grad_mixed_ref, first_query_ref, first_kv_ref,
    d_query_ref, d_kv_ref,
    masked_keys, keys_t, hides, key_sums, value_sums,
):
    d_query_ref[:, : D // 2] = first_query_ref[...]
    d_kv_ref[:, :HEAD_SIZE] = first_kv_ref[:, :HEAD_SIZE]
    d_kv_ref[:, 2 * HEAD_SIZE : 3 * HEAD_SIZE] = first_kv_ref[:, HEAD_SIZE:]
    fill_keys(kv_ref, hidden_ref, 1, masked_keys, keys_t, hides)
    backward_pairs(
        1, q_ref, kv_ref, mixed_ref, spread_ref, grad_mixed_ref, d_query_ref,
        masked_keys, keys_t, hides, key_sums, value_sums,
    )
    d_kv_ref[:, HEAD_SIZE : 2 * HEAD_SIZE] = (key_sums[...] * INV_ROOT).astype(BF)
    d_kv_ref[:, 3 * HEAD_SIZE :] = value_sums[...].astype(BF)


def greet(targets):
    barrier = pltpu.get_barrier_semaphore()
    for target in targets:
        pl.semaphore_signal(barrier, inc=1, device_id={"ctx": target}, device_id_type=MESH)
    pl.semaphore_wait(barrier, len(targets))


def send(source, target, send_sem, recv_sem, device):
    return pltpu.make_async_remote_copy(
        src_ref=source, dst_ref=target, send_sem=send_sem, recv_sem=recv_sem,
        device_id={"ctx": device}, device_id_type=MESH,
    )


def exchange_kernel(x_ref, out_ref, send_sem, recv_sem, own_sem):
    me = lax.axis_index("ctx")
    others = [lax.rem(me + d, N_CTX) for d in range(1, N_CTX)]
    greet(others)
    copies = []
    for d, other in enumerate(others):
        copy = send(x_ref.at[other], out_ref.at[me], send_sem.at[d], recv_sem.at[d], other)
        copy.start()
        copies.append(copy)
    own = pltpu.make_async_copy(x_ref.at[me], out_ref.at[me], own_sem)
    own.start()
    for copy in copies:
        copy.wait()
    own.wait()


def scatter_kernel(
    x_ref, out_ref, near, sums, landed, near_send, near_recv, send_sem, recv_sem
):
    me = lax.axis_index("ctx")
    chip, core = lax.div(me, 2), lax.rem(me, 2)
    sibling = 2 * chip + 1 - core
    chips = [lax.rem(chip + d, N_CHIP) for d in range(N_CHIP)]
    greet([*(2 * c + core for c in chips[1:]), sibling])
    order = [*range(1, N_CHIP), 0]
    shared = {}
    for d in order:
        copy = send(
            x_ref.at[2 * chips[d] + 1 - core], near.at[d], near_send.at[d], near_recv.at[d], sibling
        )
        copy.start()
        shared[d] = copy
    copies = []
    for d in order:
        shared[d].wait_recv()
        both = x_ref[2 * chips[d] + core].astype(F32) + near[d].astype(F32)
        if d == 0:
            total = both
        else:
            sums[d] = both.astype(BF)
            copy = send(
                sums.at[d], landed.at[d], send_sem.at[d], recv_sem.at[d], 2 * chips[d] + core
            )
            copy.start()
            copies.append(copy)
    for d, copy in enumerate(copies, start=1):
        copy.wait_recv()
        total = total + landed[d].astype(F32)
    out_ref[...] = total.astype(BF)
    for copy in copies:
        copy.wait_send()
    for d in order:
        shared[d].wait_send()


def dma(count):
    return pltpu.SemaphoreType.DMA((count,))


def remote(kernel, shape, scratch, number, sent):
    return pl.pallas_call(
        kernel,
        out_shape=jax.ShapeDtypeStruct(shape, BF),
        in_specs=in_vmem(1),
        out_specs=in_vmem(1)[0],
        scratch_shapes=scratch,
        compiler_params=pltpu.CompilerParams(
            collective_id=number, has_side_effects=True, vmem_limit_bytes=VMEM_LIMIT
        ),
        cost_estimate=pl.CostEstimate(flops=0, bytes_accessed=sent, transcendentals=0),
    )


def exchange(slabs, number):
    shape = (SLOTS, SLAB, WIDE)
    scratch = [dma(N_CTX - 1), dma(N_CTX - 1), pltpu.SemaphoreType.DMA]
    out = remote(exchange_kernel, shape, scratch, number, 2**26)(slabs.reshape(shape))
    return out.reshape(SLAB_ROWS, WIDE)


def scatter_sum(parts):
    blocks = parts.reshape(N_CTX, ROWS, -1)
    block = blocks.shape[1:]
    slots = pltpu.VMEM((N_CHIP, *block), BF)
    scratch = [slots, slots, slots, dma(8), dma(8), dma(8), dma(8)]
    return remote(scatter_kernel, block, scratch, 3, 2**26)(blocks)


def over_pair(array):
    return lax.ppermute(array, "dp", [(i, (i + 4) % 8) for i in range(8)])


def unfold(slab, name):
    return pl.pallas_call(
        unfold_kernel,
        out_shape=jax.ShapeDtypeStruct((SLOTS * CAP, D), BF),
        in_specs=in_vmem(1),
        out_specs=in_vmem(1)[0],
        name=name,
        **local(10**9),
    )(slab)


def per_device(
    query, key, value, span_order, expert_ids, expert_gates,
    trainable, norm_gain, upstream, expert_weights,
):
    bf_shape = lambda *s: jax.ShapeDtypeStruct(s, BF)
    half = ROWS // 2
    place = (span_order[0][:, None] * half + jnp.arange(half, dtype=jnp.int32)[None, :]).reshape(-1)
    own_place = lax.dynamic_slice_in_dim(place, lax.axis_index("ctx") * ROWS, ROWS)
    hidden = (place[:, None] > own_place[None, :]).astype(BF)
    ids, named = expert_ids[0].T, trainable[:, None]
    gain = norm_gain[None, :]
    weights = expert_weights[0].transpose(1, 0, 2)

    slab_shape = bf_shape(SLAB_ROWS, WIDE)
    sent_grads = pl.pallas_call(
        weighted_kernel, out_shape=slab_shape, in_specs=in_vmem(4), out_specs=in_vmem(1)[0],
        name="weighted", **local(10**9),
    )(ids, expert_gates[0].T, named, upstream[0])

    groups = KEY_VALUE_HEADS
    slabs = (SLOTS, SLAB, WIDE)
    quarters = (FOLDS, SLOTS, SLAB, WIDE // FOLDS)
    factor_shape = jax.ShapeDtypeStruct((SLOTS, 16, 128), F32)
    whole, grad_slabs, mixed, spread, row_slabs, factors = pl.pallas_call(
        forward_kernel,
        out_shape=(
            bf_shape(N_CTX, ROWS, 2 * groups * HEAD_SIZE),
            bf_shape(*slabs),
            bf_shape(ROWS, D),
            jax.ShapeDtypeStruct((PAIRS, 2 * ROWS), F32),
            bf_shape(*quarters),
            factor_shape,
        ),
        in_specs=in_vmem(6),
        out_specs=tuple(in_vmem(6)),
        scratch_shapes=[
            pltpu.VMEM((groups, KEYS, 2 * HEAD_SIZE), BF),
            pltpu.VMEM((groups, HEAD_SIZE, KEYS), BF),
            pltpu.VMEM((2 * ROWS, ROWS), BF),
            pltpu.VMEM((KEYS, 2 * ROWS), F32),
            pltpu.VMEM(quarters, BF),
            pltpu.VMEM((SLOTS, 16, 128), F32),
            dma(7), dma(7), dma(7), dma(7), dma(2), dma(3), dma(15), dma(15),
            pltpu.SemaphoreType.DMA((FOLDS, 15)), pltpu.SemaphoreType.DMA((FOLDS, 15)),
            dma(FOLDS), dma(15), dma(15),
        ],
        compiler_params=pltpu.CompilerParams(
            collective_id=0, has_side_effects=True, vmem_limit_bytes=VMEM_LIMIT
        ),
        cost_estimate=pl.CostEstimate(flops=2 * 10**10, bytes_accessed=2**26, transcendentals=0),
        name="attention",
    )(
        jnp.concatenate([key[0], value[0]], axis=1), sent_grads.reshape(slabs),
        query[0], hidden, ids, named,
    )
    whole = whole.reshape(KEYS, -1)
    grad_slabs = grad_slabs.reshape(SLAB_ROWS, WIDE)
    other_slabs = over_pair(grad_slabs)

    rows = pl.pallas_call(
        norm_kernel, out_shape=bf_shape(SLOTS * CAP, D), in_specs=in_vmem(3),
        out_specs=in_vmem(1)[0], name="unfold_rows", **local(10**9),
    )(
        row_slabs.reshape(FOLDS, SLAB_ROWS, WIDE // FOLDS), factors.reshape(SLOTS * 16, 128), gain
    )
    all_rows = lax.all_gather(rows, "dp", axis=0, axis_index_groups=X_GROUPS)
    grads = unfold(grad_slabs, "unfold_grads")

    mine = lax.div(lax.axis_index("dp"), 4)
    half, taken_rows = H // 2, SLOTS * CAP
    terms, products, sent_back = pl.pallas_call(
        expert_kernel,
        grid=(2,),
        out_shape=(
            bf_shape(4, 2, 2, PART, taken_rows),
            bf_shape(2, half, taken_rows),
            slab_shape,
        ),
        in_specs=[
            pl.BlockSpec(memory_space=pltpu.SMEM),
            pl.BlockSpec((taken_rows, D), lambda i: (0, 0)),
            pl.BlockSpec((taken_rows, D), lambda i: (0, 0)),
            pl.BlockSpec((3, half, D), lambda i: (0, i, 0)),
        ],
        out_specs=(
            pl.BlockSpec((4, 2, 2, PART, taken_rows), lambda i: (0, 0, 0, 0, 0)),
            pl.BlockSpec((2, half, taken_rows), lambda i: (0, 0, 0)),
            pl.BlockSpec((SLAB_ROWS, WIDE), lambda i: (0, 0)),
        ),
        scratch_shapes=[
            pltpu.VMEM((D, taken_rows), BF),
            pltpu.VMEM((D, taken_rows), BF),
            pltpu.VMEM((taken_rows, D), F32),
        ],
        name="experts",
        **local(10**10),
    )(mine[None], rows, grads, weights)

    x = lax.rem(lax.axis_index("dp"), 4)
    near_terms = [lax.dynamic_index_in_dim(terms, x, 0, keepdims=False)]
    for k in range(1, 4):
        given = lax.dynamic_index_in_dim(terms, lax.rem(x + k, 4), 0, keepdims=False)
        near_terms.append(
            lax.ppermute(given, "dp", [(i, 4 * (i // 4) + (i + k) % 4) for i in range(8)])
        )
    other_products = over_pair(products[1])

    echo = exchange(sent_back, 2)
    other_grads = unfold(other_slabs, "unfold_others")
    other_products, products, echo, *near_terms = lax.optimization_barrier(
        (other_products, products, echo, *near_terms)
    )
    across = lambda rows: pl.BlockSpec((rows, WIDE), lambda i: (0, i))
    fixed = lambda *shape: pl.BlockSpec(shape, lambda i: (0,) * len(shape))
    down = pl.pallas_call(
        down_kernel,
        grid=(FOLDS,),
        out_shape=bf_shape(half, D),
        in_specs=[across(taken_rows), across(taken_rows), *[fixed(half, taken_rows)] * 2],
        out_specs=across(half),
        name="down_terms",
        **local(4 * 10**9),
    )(grads, other_grads, products[0], other_products)
    down = lax.psum_scatter(
        down, "dp", scatter_dimension=0, tiled=True, axis_index_groups=X_GROUPS
    )

    kept_scratch = [
        pltpu.VMEM((KEYS, 2 * HEAD_SIZE), BF),
        pltpu.VMEM((HEAD_SIZE, KEYS), BF),
        pltpu.VMEM((2 * ROWS, ROWS), BF),
        pltpu.VMEM((KEYS, HEAD_SIZE), F32),
        pltpu.VMEM((KEYS, HEAD_SIZE), F32),
    ]
    first_query, first_kv, grad_mixed = pl.pallas_call(
        first_backward_kernel,
        out_shape=(bf_shape(ROWS, D // 2), bf_shape(KEYS, 2 * HEAD_SIZE), bf_shape(ROWS, D)),
        in_specs=in_vmem(10),
        out_specs=tuple(in_vmem(3)),
        scratch_shapes=[*kept_scratch, pltpu.VMEM((SLOTS * CAP, D), BF)],
        name="attention_grads_0",
        **local(2 * 10**10),
    )(query[0], whole, hidden, ids, named, gain, mixed, spread, upstream[0], echo)
    first_kv, all_rows, *near_terms = lax.optimization_barrier((first_kv, all_rows, *near_terms))
    kept, given = pl.pallas_call(
        gate_up_kernel,
        grid=(FOLDS,),
        out_shape=(bf_shape(2 * PART, D), bf_shape(2 * PART, D)),
        in_specs=[
            *[fixed(2, 2, PART, taken_rows)] * 4,
            pl.BlockSpec((4, taken_rows, WIDE), lambda i: (0, 0, i)),
        ],
        out_specs=(across(2 * PART), across(2 * PART)),
        name="gate_up_terms",
        **local(4 * 10**9),
    )(*near_terms, all_rows)
    taken = over_pair(given)
    first_query, kept = lax.optimization_barrier((first_query, kept))
    d_query, d_kv = pl.pallas_call(
        second_backward_kernel,
        out_shape=(bf_shape(ROWS, D), bf_shape(KEYS, 2 * groups * HEAD_SIZE)),
        in_specs=in_vmem(8),
        out_specs=tuple(in_vmem(2)),
        scratch_shapes=kept_scratch,
        name="attention_grads_1",
        **local(2 * 10**10),
    )(query[0], whole, hidden, mixed, spread, grad_mixed, first_query, first_kv)
    kv_sums = scatter_sum(d_kv)
    split = groups * HEAD_SIZE
    gate_up = (kept.astype(F32) + taken.astype(F32)).astype(BF)
    expert_grads = jnp.concatenate([gate_up, down], axis=0).reshape(3, PART, D)
    return (
        d_query[None],
        kv_sums[None, :, :split],
        kv_sums[None, :, split:],
        expert_grads.transpose(1, 0, 2)[None],
    )


def solution(mesh):
    in_specs = (
        P("dp", "ctx", None),
        P("dp", "ctx", None),
        P("dp", "ctx", None),
        P("dp", None),
        P("dp", "ctx", None),
        P("dp", "ctx", None),
        P(),
        P(),
        P("dp", "ctx", None),
        P("ctx", None, None, None),
    )
    out_specs = (
        P("dp", "ctx", None),
        P("dp", "ctx", None),
        P("dp", "ctx", None),
        P("ctx", "dp", None, None),
    )
    return jax.shard_map(
        per_device, mesh=mesh, in_specs=in_specs, out_specs=out_specs, check_vma=False
    )
```

time: 301 us -> 249 us (0.83)
  waiting for transfers between devices: 44 us -> 0.07 us
  starting transfers between devices: 13.6 us -> 9.08 us
  Pallas kernels: 213 us -> 209 us
  other arithmetic: 5.14 us -> 8.15 us
    ppermute x3, waiting for transfers between devices: 44 us -> 0.01 us  [over_pair(): return lax.ppermute(array, 'dp', [(i, (i + 4) % 8) for i in range(8)])]
    pallas_call x2 -> x1, Pallas kernels: 52.2 us -> 26 us  [exchange(): remote(exchange_kernel, shape, scratch, number, 2 ** 26)]
    pallas_call x6 -> x9, Pallas kernels: 137 us -> 149 us  [the longest x1 67.8 us: per_device(): pl.pallas_call(forward_kernel, out_shape=(bf_shape(N_CTX, ROWS, 2 * group...]
    pallas_call x1, Pallas kernels: 19.5 us -> 29.4 us  [scatter_sum(): return remote(scatter_kernel, block, scratch, 3, 2 ** 26)(blocks)]
    all_to_all x1 -> x0, starting transfers between devices: 7.98 us -> none  [per_device(): lax.all_to_all(sent_grads.reshape(SLOTS, SLAB, WIDE), 'ctx', split_axis=0...]
    slice x4 -> x0, local copies, waits for them, and re-layouts: 4.69 us -> none  [the longest x2 3.29 us: partial(): kept[at:at + count]]
    squeeze x0 -> x3, local copies, waits for them, and re-layouts: none -> 3.69 us  [the longest x1 1.96 us: per_device(): lax.dynamic_index_in_dim(terms, lax.rem(x + k, 4), 0, keepdims=False)]
    concatenate x1 -> x2, other arithmetic: 0.67 us -> 4.33 us  [the longest x1 2.79 us: per_device(): expert_grads = jnp.concatenate([gate_up, down], axis=0).reshape(3, PART, D)]
  transfers between devices with their start and end apart: 6 -> 8, of which waited for: 2 -> 0; matrix products, arithmetic and copies ran while one was open for 3% -> 3% of each run, Pallas kernels for 67% -> 54%
where the time goes in v1:
time: 249 us; the launch traced here: 248 us
  Pallas kernels  209 us (84%)
  between operations  14.2 us (6%)
  starting transfers between devices  9.08 us (4%)
  other arithmetic  8.15 us (3%)
  local copies, waits for them, and re-layouts  8.06 us (3%)
    pallas_call x1, Pallas kernels, per_device(): pl.pallas_call(forward_kernel, out_shape=(bf_shape(N_CTX, ROWS, 2 * group...  67.8 us
    pallas_call x1, Pallas kernels, scatter_sum(): return remote(scatter_kernel, block, scratch, 3, 2 ** 26)(blocks)  29.4 us
    pallas_call x1, Pallas kernels, exchange(): remote(exchange_kernel, shape, scratch, number, 2 ** 26)  26 us
    pallas_call x1, Pallas kernels, per_device(): pl.pallas_call(expert_kernel, grid=(2,), out_shape=(bf_shape(4, 2, 2, PAR...  22.5 us
    pallas_call x1, Pallas kernels, per_device(): pl.pallas_call(first_backward_kernel, out_shape=(bf_shape(ROWS, D // 2),...  18.9 us
    pallas_call x1, Pallas kernels, per_device(): pl.pallas_call(second_backward_kernel, out_shape=(bf_shape(ROWS, D), bf_s...  17.8 us
    pallas_call x1, Pallas kernels, per_device(): pl.pallas_call(gate_up_kernel, grid=(FOLDS,), out_shape=(bf_shape(2 * PAR...  7.3 us
    pallas_call x2, Pallas kernels, unfold(): pl.pallas_call(unfold_kernel, out_shape=jax.ShapeDtypeStruct((SLOTS * CAP...  6.26 us
  transfers between devices with their start and end apart: 8, of which 0 were waited for; matrix products, arithmetic and copies ran while one was open for 3% of the time, Pallas kernels for 54%

profile of v1, /device:TPU:1, one launch (start us, length us, event | category | flops | bytes accessed | tf_op | source)
XLA Modules:
  0.0 248.1 jit_solution(8750789829763836186)
XLA Ops:
  7.2 0.7 multiply_bitcast_fusion
  7.9 1.3 copy.14.trainable_ref
  9.2 0.1 iota_add_fusion
  9.3 0.1 add.54
  9.3 0.1 dynamic_slice.16
  9.4 1.2 compare_convert_fusion.hidden_ref
  10.6 1.5 pad_maximum_fusion.1.kv_ref
  12.1 3.8 %weighted.1 = bf16[768,1024]{1,0:T(8,128)(2,1)} custom-call(s32[8,128]{1,0:T(8,128)} %bitcast.68, f32[8,128]{1,0:T(8,128)} %bitcast.67, s32[16,1]{1,0:T(8,128)} %copy.14.trainable_ref, bf16[128,4096]{1,0:T(8,128)(2,1)} %bitcast.60), custom_call_target="tpu_custom_call" | custom-call | flops 1000000000 | bytes 4194304 | tf_op jit(solution)/shard_map/weighted/pallas_call | solution.py:598
  15.9 67.8 %attention.1 = (bf16[16,128,512]{2,1,0:T(8,128)(2,1)}, bf16[16,48,1024]{2,1,0:T(8,128)(2,1)}, bf16[128,4096]{1,0:T(8,128)(2,1)}, f32[16,256]{1,0:T(8,128)}, bf16...) custom-call(bf16[128,512]{1,0:T(8,128)(2,1)} %pad_maximum_fusion.1.kv_ref, bf16[16,48,1024]{2,1,0:T(8,128)(2,1)} %bitcast.74, ...), custom_call_target="tpu_custom_call" | custom-call | flops 20000000000 | bytes 67108864 | tf_op jit(solution)/shard_map/attention/pallas_call | solution.py:607
  83.7 3.5 %unfold_rows.1.rows_ref = bf16[192,4096]{1,0:T(8,128)(2,1)} custom-call(bf16[4,768,256]{2,1,0:T(8,128)(2,1)} %bitcast.73, f32[256,128]{1,0:T(8,128)} %bitcast.76, f32[1,4096]{1,0:T(1,128)} %bitcast.65), custom_call_target="tpu_custom_call" | custom-call | flops 1000000000 | bytes 4194304 | tf_op jit(solution)/shard_map/unfold_rows/pallas_call | solution.py:643
  87.2 1.3 copy-done.2
  88.5 2.6 %collective-permute-start.5 = (bf16[768,1024]{1,0:T(8,128)(2,1)S(1)}, bf16[768,1024]{1,0:T(8,128)(2,1)}, u32[]{:S(2)}, u32[]{:S(2)}) collective-permute-start(bf16[768,1024]{1,0:T(8,128)(2,1)S(1)} %bitcast.59), channel_id=1, source_target_pairs={{0,64},{16,80},{32,96},{48,112},{64,0},{80,16},{96,32},{112,48},{1... | collective-permute-start | bytes 4718600 | tf_op jit(solution)/shard_map/ppermute | solution.py:570
  91.1 3.1 %unfold_grads.1.grads_ref.own_ref = bf16[192,4096]{1,0:T(8,128)(2,1)} custom-call(bf16[768,1024]{1,0:T(8,128)(2,1)} %bitcast.58), custom_call_target="tpu_custom_call" | custom-call | flops 1000000000 | bytes 4194304 | tf_op jit(solution)/shard_map/unfold_grads/pallas_call | solution.py:574
  94.3 22.5 %experts.1 = (bf16[4,2,2,96,192]{4,3,2,1,0:T(8,128)(2,1)}, bf16[2,384,192]{2,1,0:T(8,128)(2,1)}, bf16[768,1024]{1,0:T(8,128)(2,1)}) custom-call(s32[1]{0:T(128)} %bitcast.14.mine_ref, bf16[192,4096]{1,0:T(8,128)(2,1)} %unfold_rows.1.rows_ref, bf16[192,4096]{1,0:T(8,128)(2,1)} %unfold_grads.1.grads_ref.own_ref, bf16[3,768,4096]{2,1,0:T(8,128)(2,1)} %bitcast.56), custom_call_target="tpu_custom_call" | custom-call | flops 10000000000 | bytes 4194304 | tf_op jit(solution)/shard_map/experts/pallas_call | solution.py:654
  116.7 0.9 slice_bitcast_fusion.1
  117.7 0.1 collective-permute-start
  117.8 2.0 dynamic-slice_bitcast_fusion
  119.8 2.5 %collective-permute-start.3 = (bf16[2,2,96,192]{3,2,1,0:T(8,128)(2,1)S(1)}, bf16[2,2,96,192]{3,2,1,0:T(8,128)(2,1)S(1)}, u32[]{:S(2)}, u32[]{:S(2)}) collective-permute-start(bf16[2,2,96,192]{3,2,1,0:T(8,128)(2,1)S(1)} %get-tuple-element.66), channel_id=1, source_target_pairs={{0,48},{16,0},{32,16},{48,32},{64,112},{80,64},{96,80},{112,96},{1... | collective-permute-start | bytes 442376 | tf_op jit(solution)/shard_map/ppermute | solution.py:687
  122.3 0.5 collective-permute-start.2
  122.8 0.6 collective-permute-start.1
  123.4 26.0 %shard_map.129 = bf16[16,48,1024]{2,1,0:T(8,128)(2,1)} custom-call(bf16[16,48,1024]{2,1,0:T(8,128)(2,1)} %bitcast.51), custom_call_target="tpu_custom_call" | custom-call | bytes 67108864 | tf_op jit(solution)/shard_map/pallas_call | solution.py:557
  149.5 0.8 slice_bitcast_fusion.own_products_ref
  150.3 3.1 %unfold_others.1.other_ref = bf16[192,4096]{1,0:T(8,128)(2,1)} custom-call(bf16[768,1024]{1,0:T(8,128)(2,1)} %collective-permute-done.5.slab_ref), custom_call_target="tpu_custom_call" | custom-call | flops 1000000000 | bytes 4194304 | tf_op jit(solution)/shard_map/unfold_others/pallas_call | solution.py:574
  153.4 5.5 %down_terms.1 = bf16[384,4096]{1,0:T(8,128)(2,1)} custom-call(bf16[192,4096]{1,0:T(8,128)(2,1)} %unfold_grads.1.grads_ref.own_ref, bf16[192,4096]{1,0:T(8,128)(2,1)} %unfold_others.1.other_ref, bf16[384,192]{1,0:T(8,128)(2,1)} %slice_bitcast_fusion.own_products_ref, bf16[384,192]{1,0:T(8,128)(2,1)} %copy-done.3), custom_call_target="tpu_custom_call" | custom-call | flops 4000000000 | bytes 4194304 | tf_op jit(solution)/shard_map/down_terms/pallas_call | solution.py:698
  158.9 18.9 %attention_grads_0.1 = (bf16[128,2048]{1,0:T(8,128)(2,1)}, bf16[2048,256]{1,0:T(8,128)(2,1)}, bf16[128,4096]{1,0:T(8,128)(2,1)}) custom-call(bf16[128,4096]{1,0:T(8,128)(2,1)} %bitcast.63, bf16[2048,512]{1,0:T(8,128)(2,1)} %bitcast.71, bf16[2048,128]{1,0:T(8,128)(2,1)} %compare_convert_fusion.hidden_ref, s32[8,128]{1,0:T(8,128)} %bitcast.70, ...), custom_call_target="tpu_custom_call" | custom-call | flops 20000000000 | bytes 4194304 | tf_op jit(solution)/shard_map/attention_grads_0/pallas_call | solution.py:718
  177.8 7.3 %gate_up_terms.1 = (bf16[192,4096]{1,0:T(8,128)(2,1)}, bf16[192,4096]{1,0:T(8,128)(2,1)}) custom-call(bf16[2,2,96,192]{3,2,1,0:T(8,128)(2,1)} %get-tuple-element.52.terms0, bf16[2,2,96,192]{3,2,1,0:T(8,128)(2,1)} %copy-done.6, bf16[2,2,96,192]{3,2,1,0:T(8,128)(2,1)} %copy-done.5, bf16[2,2,96,192]{3,2,1,0:T(8,128)(2,1)} %copy-done.4, ...), custom_call_target="tpu_custom_call" | custom-call | flops 4000000000 | bytes 4194304 | tf_op jit(solution)/shard_map/gate_up_terms/pallas_call | solution.py:728
  185.1 2.7 %collective-permute-start.4 = (bf16[192,4096]{1,0:T(8,128)(2,1)}, bf16[192,4096]{1,0:T(8,128)(2,1)}, u32[]{:S(2)}, u32[]{:S(2)}) collective-permute-start(bf16[192,4096]{1,0:T(8,128)(2,1)} %get-tuple-element.63), channel_id=1, source_target_pairs={{0,64},{16,80},{32,96},{48,112},{64,0},{80,16},{96,32},{112,48},{1... | collective-permute-start | bytes 4718600 | tf_op jit(solution)/shard_map/ppermute | solution.py:570
  187.8 17.8 %attention_grads_1.1 = (bf16[128,4096]{1,0:T(8,128)(2,1)}, bf16[2048,512]{1,0:T(8,128)(2,1)}) custom-call(bf16[128,4096]{1,0:T(8,128)(2,1)} %bitcast.64, bf16[2048,512]{1,0:T(8,128)(2,1)} %bitcast.72, bf16[2048,128]{1,0:T(8,128)(2,1)} %compare_convert_fusion.hidden_ref, bf16[128,4096]{1,0:T(8,128)(2,1)} %get-tuple-element.36.mixed_ref, ...), custom_call_target="tpu_custom_call" | custom-call | flops 20000000000 | bytes 4194304 | tf_op jit(solution)/shard_map/attention_grads_1/pallas_call | solution.py:742
  205.6 29.4 %shard_map.130 = bf16[128,512]{1,0:T(8,128)(2,1)} custom-call(bf16[16,128,512]{2,1,0:T(8,128)(2,1)} %bitcast.50), custom_call_target="tpu_custom_call" | custom-call | bytes 67108864 | tf_op jit(solution)/shard_map/pallas_call | solution.py:566
  235.0 1.5 slice_bitcast_fusion.2
  236.5 1.9 add_convert_fusion
  238.5 2.8 %pad_maximum_fusion = bf16[288,4096]{1,0:T(8,128)(2,1)} fusion(bf16[96,4096]{1,0:T(8,128)(2,1)} %reduce-scatter.2.cloned.1.call-done, bf16[192,4096]{1,0:T(8,128)(2,1)S(1)} %add_convert_fusion), kind=kLoop, calls=%fused_computation.1 | loop fusion | flops 4718592 | bytes 4718592 | tf_op jit(solution)/shard_map/concatenate | solution.py:754
  (25 shorter events, 0.2 us)
Async XLA Ops:
  7.2 170.7 %all-gather.3.cloned.1.call-start = ((), (), s32[]{:S(2)}) async-start(), calls=%async_computation.2 | async-start | bytes 7864320 | tf_op jit(solution)/shard_map/all_gather | solution.py:649
  87.1 1.4 copy-start.2
  87.2 151.3 %reduce-scatter.2.cloned.1.call-start = ((), (), s32[]{:S(2)}) async-start(), calls=%async_computation.1 | async-start | bytes 3932160 | tf_op jit(solution)/shard_map/reduce_scatter | solution.py:707
  88.5 61.7 %collective-permute-start.5 = (bf16[768,1024]{1,0:T(8,128)(2,1)S(1)}, bf16[768,1024]{1,0:T(8,128)(2,1)}, u32[]{:S(2)}, u32[]{:S(2)}) collective-permute-start(bf16[768,1024]{1,0:T(8,128)(2,1)S(1)} %bitcast.59), channel_id=1, source_target_pairs={{0,64},{16,80},{32,96},{48,112},{64,0},{80,16},{96,32},{112,48},{1... | collective-permute-start | bytes 4718600 | tf_op jit(solution)/shard_map/ppermute | solution.py:570
  117.7 31.7 %collective-permute-start = (bf16[384,192]{1,0:T(8,128)(2,1)S(1)}, bf16[384,192]{1,0:T(8,128)(2,1)S(1)}, u32[]{:S(2)}, u32[]{:S(2)}) collective-permute-start(bf16[384,192]{1,0:T(8,128)(2,1)S(1)} %slice_bitcast_fusion.1), channel_id=1, source_target_pairs={{0,64},{16,80},{32,96},{48,112},{64,0},{80,16},{96,32},{112,48},{1... | collective-permute-start | bytes 442376 | tf_op jit(solution)/shard_map/ppermute | solution.py:570
  119.8 29.6 %collective-permute-start.3 = (bf16[2,2,96,192]{3,2,1,0:T(8,128)(2,1)S(1)}, bf16[2,2,96,192]{3,2,1,0:T(8,128)(2,1)S(1)}, u32[]{:S(2)}, u32[]{:S(2)}) collective-permute-start(bf16[2,2,96,192]{3,2,1,0:T(8,128)(2,1)S(1)} %get-tuple-element.66), channel_id=1, source_target_pairs={{0,48},{16,0},{32,16},{48,32},{64,112},{80,64},{96,80},{112,96},{1... | collective-permute-start | bytes 442376 | tf_op jit(solution)/shard_map/ppermute | solution.py:687
  122.3 27.1 %collective-permute-start.2 = (bf16[2,2,96,192]{3,2,1,0:T(8,128)(2,1)S(1)}, bf16[2,2,96,192]{3,2,1,0:T(8,128)(2,1)S(1)}, u32[]{:S(2)}, u32[]{:S(2)}) collective-permute-start(bf16[2,2,96,192]{3,2,1,0:T(8,128)(2,1)S(1)} %get-tuple-element.67), channel_id=1, source_target_pairs={{0,32},{16,48},{32,0},{48,16},{64,96},{80,112},{96,64},{112,80},{1... | collective-permute-start | bytes 442376 | tf_op jit(solution)/shard_map/ppermute | solution.py:687
  122.8 26.6 %collective-permute-start.1 = (bf16[2,2,96,192]{3,2,1,0:T(8,128)(2,1)S(1)}, bf16[2,2,96,192]{3,2,1,0:T(8,128)(2,1)S(1)}, u32[]{:S(2)}, u32[]{:S(2)}) collective-permute-start(bf16[2,2,96,192]{3,2,1,0:T(8,128)(2,1)S(1)} %get-tuple-element.68), channel_id=1, source_target_pairs={{0,16},{16,32},{32,48},{48,0},{64,80},{80,96},{96,112},{112,64},{1... | collective-permute-start | bytes 442376 | tf_op jit(solution)/shard_map/ppermute | solution.py:687
  123.4 26.1 %copy-start.1 = (bf16[2,384,192]{2,1,0:T(8,128)(2,1)S(1)}, bf16[2,384,192]{2,1,0:T(8,128)(2,1)}, u32[]{:S(2)}) copy-start(bf16[2,384,192]{2,1,0:T(8,128)(2,1)} %get-tuple-element.64) | copy-start | bytes 884740
  149.4 4.0 %copy-start.3 = (bf16[384,192]{1,0:T(8,128)(2,1)}, bf16[384,192]{1,0:T(8,128)(2,1)S(1)}, u32[]{:S(2)}) copy-start(bf16[384,192]{1,0:T(8,128)(2,1)S(1)} %collective-permute-done.other_products_ref) | copy-start | bytes 442372
  149.4 4.0 %copy-start.4 = (bf16[2,2,96,192]{3,2,1,0:T(8,128)(2,1)}, bf16[2,2,96,192]{3,2,1,0:T(8,128)(2,1)S(1)}, u32[]{:S(2)}) copy-start(bf16[2,2,96,192]{3,2,1,0:T(8,128)(2,1)S(1)} %collective-permute-done.3.terms3) | copy-start | bytes 442372
  149.4 4.0 %copy-start.5 = (bf16[2,2,96,192]{3,2,1,0:T(8,128)(2,1)}, bf16[2,2,96,192]{3,2,1,0:T(8,128)(2,1)S(1)}, u32[]{:S(2)}) copy-start(bf16[2,2,96,192]{3,2,1,0:T(8,128)(2,1)S(1)} %collective-permute-done.2.terms2) | copy-start | bytes 442372
  149.4 4.0 %copy-start.6 = (bf16[2,2,96,192]{3,2,1,0:T(8,128)(2,1)}, bf16[2,2,96,192]{3,2,1,0:T(8,128)(2,1)S(1)}, u32[]{:S(2)}) copy-start(bf16[2,2,96,192]{3,2,1,0:T(8,128)(2,1)S(1)} %collective-permute-done.1.terms1) | copy-start | bytes 442372
  185.1 51.4 %collective-permute-start.4 = (bf16[192,4096]{1,0:T(8,128)(2,1)}, bf16[192,4096]{1,0:T(8,128)(2,1)}, u32[]{:S(2)}, u32[]{:S(2)}) collective-permute-start(bf16[192,4096]{1,0:T(8,128)(2,1)} %get-tuple-element.63), channel_id=1, source_target_pairs={{0,64},{16,80},{32,96},{48,112},{64,0},{80,16},{96,32},{112,48},{1... | collective-permute-start | bytes 4718600 | tf_op jit(solution)/shard_map/ppermute | solution.py:570
  205.6 30.9 %copy-start = (bf16[192,4096]{1,0:T(8,128)(2,1)S(1)}, bf16[192,4096]{1,0:T(8,128)(2,1)}, u32[]{:S(2)}) copy-start(bf16[192,4096]{1,0:T(8,128)(2,1)} %get-tuple-element.62) | copy-start | bytes 4718596
Sparse Core Ops, SparseCore 0:
  87.3 72.7 all-gather.2
  162.5 38.9 reduce-scatter.1

commit v2 on v1

v2 whole, which is shorter than its diff:
```python
import math

import jax
import jax.numpy as jnp
from jax import lax
from jax.experimental import pallas as pl
from jax.experimental.pallas import tpu as pltpu
from jax.sharding import PartitionSpec as P

D = 4096
QUERY_HEADS = 32
KEY_VALUE_HEADS = 2
HEAD_SIZE = 128
TOP = 8
CAP = 12
H = 768
N_CTX = 16
N_CHIP = 8
ROWS = 128
KEYS = 2048
SLOTS = 16
FOLDS = 4
WIDE = D // FOLDS
SLAB = CAP * FOLDS
SLAB_ROWS = SLOTS * SLAB
PAIRS = QUERY_HEADS // 2
KEY_BLOCK = 512
PART = H // 8

MASK_FILLER = -1e30
EPSILON = 1e-06
INV_ROOT = HEAD_SIZE ** (-0.5)
TO_BASE_TWO = INV_ROOT * math.log2(math.e)

X_GROUPS = [[0, 1, 2, 3], [4, 5, 6, 7]]
MESH = pl.DeviceIdType.MESH
VMEM_LIMIT = 40 * 2**20
BF = jnp.bfloat16
F32 = jnp.float32


def dot_nn(a, b):
    return lax.dot_general(a, b, (((1,), (0,)), ((), ())), preferred_element_type=F32)


def dot_nt(a, b):
    return lax.dot_general(a, b, (((1,), (1,)), ((), ())), preferred_element_type=F32)


def dot_tn(a, b):
    return lax.dot_general(a, b, (((0,), (0,)), ((), ())), preferred_element_type=F32)


def in_vmem(count):
    return [pl.BlockSpec(memory_space=pltpu.VMEM)] * count


def local(cost, limit=40):
    return dict(
        compiler_params=pltpu.CompilerParams(vmem_limit_bytes=limit * 2**20),
        cost_estimate=pl.CostEstimate(flops=cost, bytes_accessed=2**22, transcendentals=0),
    )


def expert_ranks(ids_ref, trainable_ref):
    hits = jnp.zeros((SLOTS, ROWS), F32)
    for k in range(TOP):
        hits = hits + jnp.where(ids_ref[k : k + 1, :] == trainable_ref[...], 1.0, 0.0)
    before = lax.broadcasted_iota(jnp.int32, (ROWS, ROWS), 0) < lax.broadcasted_iota(
        jnp.int32, (ROWS, ROWS), 1
    )
    rank = dot_nn(hits.astype(BF), jnp.where(before, 1.0, 0.0).astype(BF))
    return jnp.where(hits > 0.5, rank, -1.0)


def tenth(n):
    return lax.shift_right_logical(n * 5462, 16)


def slot_mask(rank, pad):
    rows = SLOTS * pad
    n = lax.broadcasted_iota(jnp.int32, (rows, SLOTS), 0)
    j = lax.broadcasted_iota(jnp.int32, (rows, SLOTS), 1)
    owner = tenth(n) if pad == CAP else lax.shift_right_logical(n, 4)
    spread = dot_nn(jnp.where(owner == j, 1.0, 0.0).astype(BF), rank.astype(BF))
    slot = n[:, :1] - pad * owner[:, :1]
    return spread == slot.astype(F32), owner


def swap_mask():
    o = lax.broadcasted_iota(jnp.int32, (4 * SLAB, 4 * SLAB), 0)
    i = lax.broadcasted_iota(jnp.int32, (4 * SLAB, 4 * SLAB), 1)
    a = sum(jnp.where(o >= SLAB * k, 1, 0) for k in range(1, 4))
    o = o - SLAB * a
    b = sum(jnp.where(o >= CAP * k, 1, 0) for k in range(1, 4))
    return jnp.where(i == SLAB * b + CAP * a + o - CAP * b, 1.0, 0.0).astype(BF)


def unfolded(slabs, swap):
    for g in range(4):
        rows = dot_nn(swap, slabs[g * 4 * SLAB : (g + 1) * 4 * SLAB])
        for a in range(FOLDS):
            yield slice(g * SLAB, (g + 1) * SLAB), a, rows[a * SLAB : (a + 1) * SLAB]


def folded(rows, swap):
    wide = rows.shape[1] // FOLDS
    slabs = []
    for g in range(4):
        at = slice(g * SLAB, (g + 1) * SLAB)
        pile = [rows[at, a * wide : (a + 1) * wide] for a in range(FOLDS)]
        slabs.append(dot_nn(swap, jnp.concatenate(pile, axis=0)).astype(BF))
    return jnp.concatenate(slabs, axis=0)


def exact(a, b):
    return lax.dot_general(
        a, b, (((1,), (0,)), ((), ())),
        precision=lax.Precision.HIGHEST, preferred_element_type=F32,
    )


def weighted_kernel(ids_ref, gates_ref, trainable_ref, up_ref, out_ref):
    rank = expert_ranks(ids_ref, trainable_ref)
    mask, owner = slot_mask(rank, CAP)
    gates = jnp.zeros((SLOTS, ROWS), F32)
    for k in range(TOP):
        same = ids_ref[k : k + 1, :] == trainable_ref[...]
        gates = gates + jnp.where(same, gates_ref[k : k + 1, :], 0.0)
    own = owner == lax.broadcasted_iota(jnp.int32, owner.shape, 1)
    gates = exact(jnp.where(own, 1.0, 0.0), gates)
    gate = jnp.sum(jnp.where(mask, gates, 0.0), axis=1, keepdims=True)
    rows = dot_nn(jnp.where(mask, 1.0, 0.0).astype(BF), up_ref[...])
    out_ref[...] = folded((gate * rows).astype(BF), swap_mask())


def two_heads(ref, pair):
    at = pl.multiple_of(pair * 2 * HEAD_SIZE, 2 * HEAD_SIZE)
    both = ref[:, pl.ds(at, 2 * HEAD_SIZE)]
    return jnp.concatenate([both[:, :HEAD_SIZE], both[:, HEAD_SIZE:]], axis=0)


def put_two_heads(ref, pair, stacked):
    at = pl.multiple_of(pair * 2 * HEAD_SIZE, 2 * HEAD_SIZE)
    ref[:, pl.ds(at, 2 * HEAD_SIZE)] = jnp.concatenate([stacked[:ROWS], stacked[ROWS:]], axis=1)


def diagonal():
    eye = lax.broadcasted_iota(jnp.int32, (ROWS, ROWS), 0) == lax.broadcasted_iota(
        jnp.int32, (ROWS, ROWS), 1
    )
    one = jnp.where(eye, MASK_FILLER, 0.0).astype(BF)
    return jnp.concatenate([one, one], axis=0)


def rms_factor(features):
    return lax.rsqrt(jnp.mean(features * features, axis=1, keepdims=True) + EPSILON)


def forward_kernel(
    kv_ref, slabs_ref, q_ref, hidden_ref, ids_ref, trainable_ref, gain_ref,
    whole_ref, mixed_ref, spread_ref, rows_ref, grads_ref,
    masked_keys, values_t, hides, scores, sent_rows, sent_factors, slabs_in, rows_in, factors_in,
    send_sem, recv_sem, pass_sem, passed_sem, near_sem, own_sem,
    slab_send, slab_recv, row_send, row_recv, row_own, factor_send, factor_recv,
):
    me = lax.axis_index("ctx")
    chip, core = lax.div(me, 2), lax.rem(me, 2)
    sibling = 2 * chip + 1 - core
    far = [2 * lax.rem(chip + d, N_CHIP) + core for d in range(1, N_CHIP)]
    others = [lax.rem(me + d, N_CTX) for d in range(1, N_CTX)]
    greet(others)
    copies = []
    for d, other in enumerate(far):
        copy = send(kv_ref, whole_ref.at[me], send_sem.at[d], recv_sem.at[d], other)
        copy.start()
        copies.append(copy)
    near = send(kv_ref, whole_ref.at[me], near_sem.at[0], near_sem.at[1], sibling)
    near.start()
    own = pltpu.make_async_copy(kv_ref, whole_ref.at[me], own_sem.at[0])
    own.start()

    mask, _ = slot_mask(expert_ranks(ids_ref, trainable_ref), CAP)
    mask = jnp.where(mask, 1.0, 0.0).astype(BF)
    swap = swap_mask()
    hides[...] = diagonal()
    for g in range(KEY_VALUE_HEADS):
        masked_keys[g, :, HEAD_SIZE:] = hidden_ref[...]

    passed = []
    for d in range(1, N_CHIP):
        source = 2 * lax.rem(chip + N_CHIP - d, N_CHIP) + core
        copies[d - 1].wait_recv()
        copy = send(
            whole_ref.at[source], whole_ref.at[source],
            pass_sem.at[d - 1], passed_sem.at[d - 1], sibling,
        )
        copy.start()
        passed.append(copy)
    for copy in copies:
        copy.wait_send()
    near.wait()
    own.wait()
    for copy in passed:
        copy.wait()

    slabs = []
    for d, other in enumerate(others):
        copy = send(
            slabs_ref.at[other], slabs_in.at[me], slab_send.at[d], slab_recv.at[d], other
        )
        copy.start()
        slabs.append(copy)
    own_slab = pltpu.make_async_copy(slabs_ref.at[me], slabs_in.at[me], own_sem.at[1])
    own_slab.start()

    for g in range(KEY_VALUE_HEADS):
        at = g * HEAD_SIZE
        keys = whole_ref[:, :, at : at + HEAD_SIZE].reshape(KEYS, HEAD_SIZE)
        masked_keys[g, :, :HEAD_SIZE] = keys
        at = (KEY_VALUE_HEADS + g) * HEAD_SIZE
        values_t[g] = whole_ref[:, :, at : at + HEAD_SIZE].reshape(KEYS, HEAD_SIZE).T

    def step(pair, carry):
        g = lax.div(pair, PAIRS // KEY_VALUE_HEADS)
        queries = jnp.concatenate([two_heads(q_ref, pair), hides[...]], axis=1)
        peak = None
        for b in range(KEYS // KEY_BLOCK):
            rows = slice(b * KEY_BLOCK, (b + 1) * KEY_BLOCK)
            block = dot_nt(masked_keys[g, rows, :], queries)
            scores[rows, :] = block
            top = jnp.max(block, axis=0, keepdims=True)
            peak = top if peak is None else jnp.maximum(peak, top)
        total, out = None, None
        for b in range(KEYS // KEY_BLOCK):
            rows = slice(b * KEY_BLOCK, (b + 1) * KEY_BLOCK)
            exps = jnp.exp2((scores[rows, :] - peak) * TO_BASE_TWO)
            part = jnp.sum(exps, axis=0, keepdims=True)
            piece = dot_nn(values_t[g, :, rows], exps.astype(BF))
            total = part if total is None else total + part
            out = piece if out is None else out + piece
        put_two_heads(mixed_ref, pair, (out / total).T.astype(BF))
        spread_ref[pl.ds(pair, 1), :] = peak * TO_BASE_TWO + jnp.log2(total)
        return carry

    def row_copies(f):
        return [
            send(
                sent_rows.at[f, other], rows_in.at[f, me],
                row_send.at[f, d], row_recv.at[f, d], other,
            )
            for d, other in enumerate(others)
        ]

    def own_rows(f):
        return pltpu.make_async_copy(sent_rows.at[f, me], rows_in.at[f, me], row_own.at[f])

    def quarter(f, carry):
        lax.fori_loop(f * (PAIRS // FOLDS), (f + 1) * (PAIRS // FOLDS), step, 0)
        columns = mixed_ref[:, pl.ds(pl.multiple_of(f * WIDE, WIDE), WIDE)]
        picked = folded(dot_nn(mask, columns).astype(BF), swap)
        sent_rows[f] = picked.reshape(SLOTS, SLAB, WIDE // FOLDS)
        for copy in row_copies(f):
            copy.start()
        own_rows(f).start()
        return carry

    lax.fori_loop(0, FOLDS, quarter, 0)

    features = mixed_ref[...].astype(F32)
    factor = jnp.broadcast_to(rms_factor(features), (ROWS, 128))
    padded, _ = slot_mask(expert_ranks(ids_ref, trainable_ref), 16)
    picked = exact(jnp.where(padded, 1.0, 0.0), factor)
    sent_factors[...] = picked.reshape(SLOTS, 16, 128)
    factors = []
    for d, other in enumerate(others):
        copy = send(
            sent_factors.at[other], factors_in.at[me], factor_send.at[d], factor_recv.at[d], other
        )
        copy.start()
        factors.append(copy)
    own_factor = pltpu.make_async_copy(sent_factors.at[me], factors_in.at[me], own_sem.at[2])
    own_factor.start()

    for copy in slabs:
        copy.wait()
    own_slab.wait()
    for rows, a, values in unfolded(slabs_in[...].reshape(SLAB_ROWS, WIDE), swap):
        grads_ref[rows, a * WIDE : (a + 1) * WIDE] = values.astype(BF)

    narrow = WIDE // FOLDS

    def finish(f, carry):
        for copy in row_copies(f):
            copy.wait()
        own_rows(f).wait()
        for rows, a, values in unfolded(rows_in[f].reshape(SLAB_ROWS, narrow), swap):
            at = pl.multiple_of(f * WIDE + a * narrow, narrow)
            rows_ref[rows, pl.ds(at, narrow)] = values.astype(BF)
        return carry

    lax.fori_loop(0, FOLDS, finish, 0)
    for copy in factors:
        copy.wait()
    own_factor.wait()
    n = lax.broadcasted_iota(jnp.int32, (SLOTS * CAP, SLOTS * 16), 0)
    m = lax.broadcasted_iota(jnp.int32, (SLOTS * CAP, SLOTS * 16), 1)
    kept = jnp.where(m == n + (16 - CAP) * tenth(n), 1.0, 0.0)
    factor = exact(kept, factors_in[...].reshape(SLOTS * 16, 128))[:, :1]
    rows_ref[...] = (rows_ref[...].astype(F32) * factor * gain_ref[...]).astype(BF)


def expert_kernel(
    mine_ref, rows_ref, grads_ref, w_hbm_ref, terms_ref, products_ref, back_ref,
    routed_t, weighted_t, returned, w_ref, w_sem,
):
    loads = {}
    for step in range(2):
        for i in range(3):
            units = slice(step * (H // 2), (step + 1) * (H // 2))
            loads[step, i] = pltpu.make_async_copy(
                w_hbm_ref.at[i, units], w_ref.at[i, units], w_sem.at[step, i]
            )
            loads[step, i].start()
    routed_t[...] = rows_ref[...].T
    weighted_t[...] = grads_ref[...].T
    half = H // 2
    for step in range(2):
        units = slice(step * half, (step + 1) * half)
        loads[step, 0].wait()
        gate_in = dot_nn(w_ref[0, units, :], routed_t[...])
        loads[step, 1].wait()
        up_in = dot_nn(w_ref[1, units, :], routed_t[...])
        loads[step, 2].wait()
        back = dot_nn(w_ref[2, units, :], weighted_t[...])
        sigma = jax.nn.sigmoid(gate_in)
        activated = gate_in * sigma
        grad_gate = (back * up_in * sigma * (1.0 + gate_in * (1.0 - sigma))).astype(BF)
        grad_up = (back * activated).astype(BF)
        place = lax.rem(step + mine_ref[0], 2)
        products_ref[place] = (activated * up_in).astype(BF)
        for x in range(4):
            terms_ref[x, place, 0] = grad_gate[x * PART : (x + 1) * PART]
            terms_ref[x, place, 1] = grad_up[x * PART : (x + 1) * PART]
        grad_gate, grad_up = grad_gate.T, grad_up.T
        for f in range(FOLDS):
            at = slice(f * WIDE, (f + 1) * WIDE)
            part = dot_nn(grad_gate, w_ref[0, units, at]) + dot_nn(grad_up, w_ref[1, units, at])
            if step == 0:
                returned[:, at] = part
            else:
                returned[:, at] += part
    back_ref[...] = folded(returned[...].astype(BF), swap_mask())


def down_kernel(own_ref, other_ref, own_products_ref, other_products_ref, out_ref):
    out_ref[...] = (
        dot_nn(own_products_ref[0], own_ref[...])
        + dot_nn(other_products_ref[...], other_ref[...])
    ).astype(BF)


def gate_up_kernel(terms_ref, rows_ref, kept_ref, given_ref):
    total = None
    for k in range(4):
        left = terms_ref[k].reshape(4 * PART, SLOTS * CAP)
        part = dot_nn(left, rows_ref[k])
        total = part if total is None else total + part
    kept_ref[...] = total[: 2 * PART].astype(BF)
    given_ref[...] = total[2 * PART :].astype(BF)


def finish_kernel(kept_ref, taken_ref, down_ref, out_ref):
    for i in range(2):
        at = slice(i * PART, (i + 1) * PART)
        out_ref[i] = (kept_ref[at].astype(F32) + taken_ref[at].astype(F32)).astype(BF)
    out_ref[2] = down_ref[...]


def fill_keys(kv_ref, hidden_ref, g, masked_keys, keys_t, hides):
    keys = kv_ref[:, g * HEAD_SIZE : (g + 1) * HEAD_SIZE]
    masked_keys[:, :HEAD_SIZE] = keys
    masked_keys[:, HEAD_SIZE:] = hidden_ref[...]
    keys_t[...] = keys.T
    hides[...] = diagonal()


def backward_pairs(
    g, first, last, q_ref, kv_ref, mixed_ref, spread_ref, grad_mixed_ref, d_query_ref,
    masked_keys, keys_t, hides, key_sums, value_sums,
):
    at = (KEY_VALUE_HEADS + g) * HEAD_SIZE

    def step(pair, carry):
        plain = two_heads(q_ref, pair)
        queries = jnp.concatenate([plain, hides[...]], axis=1)
        grads = two_heads(grad_mixed_ref, pair)
        products = grads.astype(F32) * two_heads(mixed_ref, pair).astype(F32)
        delta = jnp.sum(products.T, axis=0, keepdims=True)
        spread = spread_ref[pl.ds(pair, 1), :]
        d_query = None
        for b in range(KEYS // KEY_BLOCK):
            rows = slice(b * KEY_BLOCK, (b + 1) * KEY_BLOCK)
            values = kv_ref[rows, at : at + HEAD_SIZE]
            raw = dot_nt(masked_keys[rows, :], queries)
            probs = jnp.exp2(raw * TO_BASE_TWO - spread)
            pushed = dot_nt(values, grads)
            slopes = (probs * (pushed - delta)).astype(BF)
            value_sums[rows, :] += dot_nn(probs.astype(BF), grads)
            key_sums[rows, :] += dot_nn(slopes, plain)
            piece = dot_nn(keys_t[:, rows], slopes)
            d_query = piece if d_query is None else d_query + piece
        put_two_heads(d_query_ref, pair, (d_query * INV_ROOT).T.astype(BF))
        return carry

    lax.fori_loop(first, last, step, 0)


def first_backward_kernel(
    q_ref, kv_ref, hidden_ref, ids_ref, trainable_ref, gain_ref,
    mixed_ref, spread_ref, up_ref, echo_ref,
    d_query_ref, d_kv_ref, grad_mixed_ref,
    masked_keys, keys_t, hides, key_sums, value_sums, echoed,
):
    mask, _ = slot_mask(expert_ranks(ids_ref, trainable_ref), CAP)
    mask = jnp.where(mask, 1.0, 0.0).astype(BF)
    for rows, a, values in unfolded(echo_ref[...], swap_mask()):
        echoed[rows, a * WIDE : (a + 1) * WIDE] = values.astype(BF)
    features = mixed_ref[...].astype(F32)
    factor = rms_factor(features)
    gradnorm = gain_ref[...] * dot_tn(mask, echoed[...])
    across = jnp.mean(gradnorm * features, axis=1, keepdims=True)
    grad_mixed_ref[...] = (
        up_ref[...].astype(F32)
        + factor * gradnorm
        - features * (factor * factor * factor) * across
    ).astype(BF)
    fill_keys(kv_ref, hidden_ref, 0, masked_keys, keys_t, hides)
    key_sums[...] = jnp.zeros_like(key_sums)
    value_sums[...] = jnp.zeros_like(value_sums)
    backward_pairs(
        0, 0, PAIRS // 2, q_ref, kv_ref, mixed_ref, spread_ref, grad_mixed_ref, d_query_ref,
        masked_keys, keys_t, hides, key_sums, value_sums,
    )
    d_kv_ref[:, :HEAD_SIZE] = (key_sums[...] * INV_ROOT).astype(BF)
    d_kv_ref[:, HEAD_SIZE:] = value_sums[...].astype(BF)


def greet(targets):
    barrier = pltpu.get_barrier_semaphore()
    for target in targets:
        pl.semaphore_signal(barrier, inc=1, device_id={"ctx": target}, device_id_type=MESH)
    pl.semaphore_wait(barrier, len(targets))


def send(source, target, send_sem, recv_sem, device):
    return pltpu.make_async_remote_copy(
        src_ref=source, dst_ref=target, send_sem=send_sem, recv_sem=recv_sem,
        device_id={"ctx": device}, device_id_type=MESH,
    )


def second_backward_kernel(
    q_ref, kv_ref, hidden_ref, mixed_ref, spread_ref, grad_mixed_ref, first_query_ref, first_kv_ref,
    d_query_ref, key_out_ref, value_out_ref,
    masked_keys, keys_t, hides, key_sums, value_sums,
    d_kv, near, sums, landed, near_send, near_recv, send_sem, recv_sem,
):
    me = lax.axis_index("ctx")
    chip, core = lax.div(me, 2), lax.rem(me, 2)
    sibling = 2 * chip + 1 - core
    chips = [lax.rem(chip + d, N_CHIP) for d in range(N_CHIP)]
    order = [*range(1, N_CHIP), 0]
    greet([*(2 * c + core for c in chips[1:]), sibling])

    def share(g, blocks):
        copies = {}
        for d in order:
            copies[d] = send(
                blocks.at[2 * chips[d] + 1 - core], near.at[g, d],
                near_send.at[g, d], near_recv.at[g, d], sibling,
            )
            copies[d].start()
        return copies

    def cross(g, blocks, shared):
        copies = []
        for d in order:
            shared[d].wait_recv()
            both = blocks[2 * chips[d] + core].astype(F32) + near[g, d].astype(F32)
            sums[g, d] = both.astype(BF)
            if d:
                copy = send(
                    sums.at[g, d], landed.at[g, d], send_sem.at[g, d], recv_sem.at[g, d],
                    2 * chips[d] + core,
                )
                copy.start()
                copies.append(copy)
        return copies

    def total(g, copies):
        result = sums[g, 0].astype(F32)
        for d, copy in enumerate(copies, start=1):
            copy.wait_recv()
            result = result + landed[g, d].astype(F32)
        at = slice(g * HEAD_SIZE, (g + 1) * HEAD_SIZE)
        key_out_ref[:, at] = result[:, :HEAD_SIZE].astype(BF)
        value_out_ref[:, at] = result[:, HEAD_SIZE:].astype(BF)

    def pairs(first, last):
        backward_pairs(
            1, first, last, q_ref, kv_ref, mixed_ref, spread_ref, grad_mixed_ref, d_query_ref,
            masked_keys, keys_t, hides, key_sums, value_sums,
        )

    shared_0 = share(0, first_kv_ref)
    d_query_ref[:, : D // 2] = first_query_ref[...]
    fill_keys(kv_ref, hidden_ref, 1, masked_keys, keys_t, hides)
    key_sums[...] = jnp.zeros_like(key_sums)
    value_sums[...] = jnp.zeros_like(value_sums)
    pairs(PAIRS // 2, PAIRS // 2 + 2)
    copies_0 = cross(0, first_kv_ref, shared_0)
    pairs(PAIRS // 2 + 2, PAIRS)
    d_kv[:, :, :HEAD_SIZE] = (
        (key_sums[...] * INV_ROOT).astype(BF).reshape(N_CTX, ROWS, HEAD_SIZE)
    )
    d_kv[:, :, HEAD_SIZE:] = value_sums[...].astype(BF).reshape(N_CTX, ROWS, HEAD_SIZE)
    shared_1 = share(1, d_kv)
    copies_1 = cross(1, d_kv, shared_1)
    total(0, copies_0)
    total(1, copies_1)
    for copy in copies_0 + copies_1:
        copy.wait_send()
    for d in order:
        shared_0[d].wait_send()
        shared_1[d].wait_send()


def return_kernel(
    x_ref, terms_ref, products_ref, out_ref, terms_out_ref, products_out_ref,
    send_sem, recv_sem, term_send, term_recv, pair_sem, own_sem,
):
    me, dp = lax.axis_index("ctx"), lax.axis_index("dp")
    x = lax.rem(dp, 4)
    others = [lax.rem(me + d, N_CTX) for d in range(1, N_CTX)]
    line = [lax.rem(x + k, 4) for k in range(1, 4)]
    pair = lax.rem(dp + 4, 8)
    barrier = pltpu.get_barrier_semaphore()
    for other in others:
        pl.semaphore_signal(barrier, inc=1, device_id={"ctx": other}, device_id_type=MESH)
    for other in [dp - x + k for k in line] + [pair]:
        pl.semaphore_signal(barrier, inc=1, device_id={"dp": other}, device_id_type=MESH)
    pl.semaphore_wait(barrier, N_CTX + 3)
    copies = []
    for d, other in enumerate(others):
        copies.append(
            send(x_ref.at[other], out_ref.at[me], send_sem.at[d], recv_sem.at[d], other)
        )
    for d, k in enumerate(line):
        copies.append(
            pltpu.make_async_remote_copy(
                src_ref=terms_ref.at[k], dst_ref=terms_out_ref.at[x],
                send_sem=term_send.at[d], recv_sem=term_recv.at[d],
                device_id={"dp": dp - x + k}, device_id_type=MESH,
            )
        )
    copies.append(
        pltpu.make_async_remote_copy(
            src_ref=products_ref.at[1], dst_ref=products_out_ref,
            send_sem=pair_sem.at[0], recv_sem=pair_sem.at[1],
            device_id={"dp": pair}, device_id_type=MESH,
        )
    )
    copies.append(pltpu.make_async_copy(x_ref.at[me], out_ref.at[me], own_sem.at[0]))
    copies.append(pltpu.make_async_copy(terms_ref.at[x], terms_out_ref.at[x], own_sem.at[1]))
    for copy in copies:
        copy.start()
    for copy in copies:
        copy.wait()


def dma(count):
    return pltpu.SemaphoreType.DMA((count,))


def over_pair(array):
    return lax.ppermute(array, "dp", [(i, (i + 4) % 8) for i in range(8)])


def per_device(
    query, key, value, span_order, expert_ids, expert_gates,
    trainable, norm_gain, upstream, expert_weights,
):
    bf_shape = lambda *s: jax.ShapeDtypeStruct(s, BF)
    half = ROWS // 2
    place = (span_order[0][:, None] * half + jnp.arange(half, dtype=jnp.int32)[None, :]).reshape(-1)
    own_place = lax.dynamic_slice_in_dim(place, lax.axis_index("ctx") * ROWS, ROWS)
    hidden = (place[:, None] > own_place[None, :]).astype(BF)
    ids, named = expert_ids[0].T, trainable[:, None]
    gain = norm_gain[None, :]
    weights = expert_weights[0].transpose(1, 0, 2)

    slab_shape = bf_shape(SLAB_ROWS, WIDE)
    sent_grads = pl.pallas_call(
        weighted_kernel, out_shape=slab_shape, in_specs=in_vmem(4), out_specs=in_vmem(1)[0],
        name="weighted", **local(10**9, 24),
    )(ids, expert_gates[0].T, named, upstream[0])

    groups = KEY_VALUE_HEADS
    slabs = (SLOTS, SLAB, WIDE)
    quarters = (FOLDS, SLOTS, SLAB, WIDE // FOLDS)
    whole, mixed, spread, rows, grads = pl.pallas_call(
        forward_kernel,
        out_shape=(
            bf_shape(N_CTX, ROWS, 2 * groups * HEAD_SIZE),
            bf_shape(ROWS, D),
            jax.ShapeDtypeStruct((PAIRS, 2 * ROWS), F32),
            bf_shape(SLOTS * CAP, D),
            bf_shape(SLOTS * CAP, D),
        ),
        in_specs=in_vmem(7),
        out_specs=tuple(in_vmem(5)),
        scratch_shapes=[
            pltpu.VMEM((groups, KEYS, 2 * HEAD_SIZE), BF),
            pltpu.VMEM((groups, HEAD_SIZE, KEYS), BF),
            pltpu.VMEM((2 * ROWS, ROWS), BF),
            pltpu.VMEM((KEYS, 2 * ROWS), F32),
            pltpu.VMEM(quarters, BF),
            pltpu.VMEM((SLOTS, 16, 128), F32),
            pltpu.VMEM(slabs, BF),
            pltpu.VMEM(quarters, BF),
            pltpu.VMEM((SLOTS, 16, 128), F32),
            dma(7), dma(7), dma(7), dma(7), dma(2), dma(3), dma(15), dma(15),
            pltpu.SemaphoreType.DMA((FOLDS, 15)), pltpu.SemaphoreType.DMA((FOLDS, 15)),
            dma(FOLDS), dma(15), dma(15),
        ],
        compiler_params=pltpu.CompilerParams(
            collective_id=0, has_side_effects=True, vmem_limit_bytes=36 * 2**20
        ),
        cost_estimate=pl.CostEstimate(flops=2 * 10**10, bytes_accessed=2**26, transcendentals=0),
        name="attention",
    )(
        jnp.concatenate([key[0], value[0]], axis=1), sent_grads.reshape(slabs),
        query[0], hidden, ids, named, gain,
    )
    whole = whole.reshape(KEYS, -1)
    other_grads = over_pair(grads)
    all_rows = lax.all_gather(rows, "dp", axis=0, axis_index_groups=X_GROUPS)

    mine = lax.div(lax.axis_index("dp"), 4)
    half, taken_rows = H // 2, SLOTS * CAP
    term_shape = (4, 2, 2, PART, taken_rows)
    terms, products, sent_back = pl.pallas_call(
        expert_kernel,
        out_shape=(bf_shape(*term_shape), bf_shape(2, half, taken_rows), slab_shape),
        in_specs=[
            pl.BlockSpec(memory_space=pltpu.SMEM),
            *in_vmem(2),
            pl.BlockSpec(memory_space=pl.ANY),
        ],
        out_specs=tuple(in_vmem(3)),
        scratch_shapes=[
            pltpu.VMEM((D, taken_rows), BF),
            pltpu.VMEM((D, taken_rows), BF),
            pltpu.VMEM((taken_rows, D), F32),
            pltpu.VMEM((3, H, D), BF),
            pltpu.SemaphoreType.DMA((2, 3)),
        ],
        name="experts",
        **local(10**10),
    )(mine[None], rows, grads, weights)

    echo, near_terms, other_products = pl.pallas_call(
        return_kernel,
        out_shape=(bf_shape(*slabs), bf_shape(*term_shape), bf_shape(half, taken_rows)),
        in_specs=in_vmem(3),
        out_specs=tuple(in_vmem(3)),
        scratch_shapes=[dma(15), dma(15), dma(3), dma(3), dma(2), dma(2)],
        compiler_params=pltpu.CompilerParams(
            collective_id=1, has_side_effects=True, vmem_limit_bytes=VMEM_LIMIT
        ),
        cost_estimate=pl.CostEstimate(flops=0, bytes_accessed=2**26, transcendentals=0),
        name="return",
    )(sent_back.reshape(slabs), terms, products)
    echo = echo.reshape(SLAB_ROWS, WIDE)

    across = lambda rows: pl.BlockSpec((rows, WIDE), lambda i: (0, i))
    fixed = lambda *shape: pl.BlockSpec(shape, lambda i: (0,) * len(shape))
    down = pl.pallas_call(
        down_kernel,
        grid=(FOLDS,),
        out_shape=bf_shape(half, D),
        in_specs=[
            across(taken_rows), across(taken_rows),
            pl.BlockSpec((1, half, taken_rows), lambda i: (0, 0, 0)), fixed(half, taken_rows),
        ],
        out_specs=across(half),
        name="down_terms",
        **local(4 * 10**9),
    )(grads, other_grads, products, other_products)
    down, all_rows, near_terms = lax.optimization_barrier((down, all_rows, near_terms))
    down = lax.psum_scatter(
        down, "dp", scatter_dimension=0, tiled=True, axis_index_groups=X_GROUPS
    )

    kept, given = pl.pallas_call(
        gate_up_kernel,
        grid=(FOLDS,),
        out_shape=(bf_shape(2 * PART, D), bf_shape(2 * PART, D)),
        in_specs=[
            fixed(*term_shape),
            pl.BlockSpec((4, taken_rows, WIDE), lambda i: (0, 0, i)),
        ],
        out_specs=(across(2 * PART), across(2 * PART)),
        name="gate_up_terms",
        **local(4 * 10**9),
    )(near_terms, all_rows)
    taken = over_pair(given)
    echo, kept = lax.optimization_barrier((echo, kept))
    kept_scratch = [
        pltpu.VMEM((KEYS, 2 * HEAD_SIZE), BF),
        pltpu.VMEM((HEAD_SIZE, KEYS), BF),
        pltpu.VMEM((2 * ROWS, ROWS), BF),
        pltpu.VMEM((KEYS, HEAD_SIZE), F32),
        pltpu.VMEM((KEYS, HEAD_SIZE), F32),
    ]
    first_query, first_kv, grad_mixed = pl.pallas_call(
        first_backward_kernel,
        out_shape=(bf_shape(ROWS, D // 2), bf_shape(KEYS, 2 * HEAD_SIZE), bf_shape(ROWS, D)),
        in_specs=in_vmem(10),
        out_specs=tuple(in_vmem(3)),
        scratch_shapes=[*kept_scratch, pltpu.VMEM((SLOTS * CAP, D), BF)],
        name="attention_grads_0",
        **local(2 * 10**10),
    )(query[0], whole, hidden, ids, named, gain, mixed, spread, upstream[0], echo)
    blocks = (N_CTX, ROWS, 2 * HEAD_SIZE)
    slots = pltpu.VMEM((groups, N_CHIP, ROWS, 2 * HEAD_SIZE), BF)
    dmas = pltpu.SemaphoreType.DMA((groups, N_CHIP))
    d_query, d_key, d_value = pl.pallas_call(
        second_backward_kernel,
        out_shape=(bf_shape(ROWS, D), *[bf_shape(ROWS, groups * HEAD_SIZE)] * 2),
        in_specs=in_vmem(8),
        out_specs=tuple(in_vmem(3)),
        scratch_shapes=[
            *kept_scratch, pltpu.VMEM(blocks, BF), slots, slots, slots, dmas, dmas, dmas, dmas,
        ],
        compiler_params=pltpu.CompilerParams(
            collective_id=2, has_side_effects=True, vmem_limit_bytes=VMEM_LIMIT
        ),
        cost_estimate=pl.CostEstimate(flops=2 * 10**10, bytes_accessed=2**26, transcendentals=0),
        name="attention_grads_1",
    )(
        query[0], whole, hidden, mixed, spread, grad_mixed, first_query, first_kv.reshape(blocks)
    )
    expert_grads = pl.pallas_call(
        finish_kernel, out_shape=bf_shape(3, PART, D), in_specs=in_vmem(3),
        out_specs=in_vmem(1)[0], name="expert_grads", **local(10**7),
    )(kept, taken, down)
    return (
        d_query[None],
        d_key[None],
        d_value[None],
        expert_grads.transpose(1, 0, 2)[None],
    )


def solution(mesh):
    in_specs = (
        P("dp", "ctx", None),
        P("dp", "ctx", None),
        P("dp", "ctx", None),
        P("dp", None),
        P("dp", "ctx", None),
        P("dp", "ctx", None),
        P(),
        P(),
        P("dp", "ctx", None),
        P("ctx", None, None, None),
    )
    out_specs = (
        P("dp", "ctx", None),
        P("dp", "ctx", None),
        P("dp", "ctx", None),
        P("ctx", "dp", None, None),
    )
    return jax.shard_map(
        per_device, mesh=mesh, in_specs=in_specs, out_specs=out_specs, check_vma=False
    )
```

time: 249 us -> 227 us (0.912)
  Pallas kernels: 209 us -> 179 us
  waiting for transfers between devices: 0.07 us -> 8.33 us
  local copies, waits for them, and re-layouts: 8.06 us -> 16.1 us
  other arithmetic: 8.15 us -> 2.1 us
  starting transfers between devices: 9.08 us -> 5.72 us
    pallas_call x7 -> x4, Pallas kernels: 105 us -> 89.5 us  [the longest x1 35.2 us: per_device(): pl.pallas_call(return_kernel, out_shape=(bf_shape(*slabs), bf_shape(*term...]
    unnamed x14 -> x47, local copies, waits for them, and re-layouts: 1.36 us -> 15.2 us
    all_gather x1, waiting for transfers between devices: 0.01 us -> 8.29 us  [per_device(): all_rows = lax.all_gather(rows, 'dp', axis=0, axis_index_groups=X_GROUPS)]
    pallas_call x1, Pallas kernels: 18.9 us -> 14.2 us  [per_device(): pl.pallas_call(first_backward_kernel, out_shape=(bf_shape(ROWS, D // 2),...]
    squeeze x3 -> x0, local copies, waits for them, and re-layouts: 3.69 us -> none  [the longest x1 1.96 us: per_device(): lax.dynamic_index_in_dim(terms, lax.rem(x + k, 4), 0, keepdims=False)]
    ppermute x3 -> x0, starting transfers between devices: 3.62 us -> none  [per_device(): lax.ppermute(given, 'dp', [(i, 4 * (i // 4) + (i + k) % 4) for i in range...]
    concatenate x1 -> x0, other arithmetic: 2.79 us -> none  [per_device(): expert_grads = jnp.concatenate([gate_up, down], axis=0).reshape(3, PART, D)]
    pallas_call x1, Pallas kernels: 7.3 us -> 4.52 us  [per_device(): pl.pallas_call(gate_up_kernel, grid=(FOLDS,), out_shape=(bf_shape(2 * PAR...]
  transfers between devices with their start and end apart: 8 -> 4, of which waited for: 0 -> 1; matrix products, arithmetic and copies ran while one was open for 3% -> 0% of each run, Pallas kernels for 54% -> 49%
where the time goes in v2:
time: 227 us; the launch traced here: 225 us
  Pallas kernels  179 us (79%)
  local copies, waits for them, and re-layouts  16.1 us (7%)
  between operations  14.2 us (6%)
  waiting for transfers between devices  8.33 us (4%)
  starting transfers between devices  5.72 us (3%)
    pallas_call x1, Pallas kernels, per_device(): pl.pallas_call(forward_kernel, out_shape=(bf_shape(N_CTX, ROWS, 2 * group...  65.2 us
    pallas_call x1, Pallas kernels, per_device(): pl.pallas_call(return_kernel, out_shape=(bf_shape(*slabs), bf_shape(*term...  35.2 us
    pallas_call x1, Pallas kernels, per_device(): pl.pallas_call(second_backward_kernel, out_shape=(bf_shape(ROWS, D), *[bf...  31.8 us
    pallas_call x1, Pallas kernels, per_device(): pl.pallas_call(expert_kernel, out_shape=(bf_shape(*term_shape), bf_shape(...  20.7 us
    unnamed x47, local copies, waits for them, and re-layouts  15.2 us
    pallas_call x1, Pallas kernels, per_device(): pl.pallas_call(first_backward_kernel, out_shape=(bf_shape(ROWS, D // 2),...  14.2 us
    all_gather x1, waiting for transfers between devices, per_device(): all_rows = lax.all_gather(rows, 'dp', axis=0, axis_index_groups=X_GROUPS)  8.29 us
    ppermute x2, starting transfers between devices, over_pair(): return lax.ppermute(array, 'dp', [(i, (i + 4) % 8) for i in range(8)])  5.65 us
  transfers between devices with their start and end apart: 4, of which 1 were waited for; matrix products, arithmetic and copies ran while one was open for 0% of the time, Pallas kernels for 49%

profile of v2, /device:TPU:1, one launch (start us, length us, event | category | flops | bytes accessed | tf_op | source)
XLA Modules:
  0.0 225.0 jit_solution(18138341384304804612)
XLA Ops:
  7.2 0.7 copy.14.trainable_ref
  7.9 0.7 multiply_bitcast_fusion
  8.6 0.1 iota_add_fusion
  8.8 0.1 dynamic_slice.3
  8.8 0.3 compare_convert_fusion.hidden_ref
  9.2 1.0 pad_maximum_fusion.kv_ref
  10.2 1.2 copy-done.8
  11.4 0.7 copy-done.15
  12.1 0.7 copy-done.16
  12.8 1.3 weighted.1
  14.2 65.2 %attention.1 = (bf16[16,128,512]{2,1,0:T(8,128)(2,1)S(1)}, bf16[128,4096]{1,0:T(8,128)(2,1)S(1)}, f32[16,256]{1,0:T(8,128)S(1)}, bf16[192,4096]{1,0:T(8,128)(2,1)}, bf16[192,4096]{1,0:T(8,128)(2,1)S(1)}) custom-call(bf16[128,512]{1,0:T(8,128)(2,1)S(1)} %pad_maximum_fusion.kv_ref, bf16[16,48,1024]{2,1,0:T(8,128)(2,1)S(1)} %bitcast.49, ...), custom_call_target="tpu_custom_call" | custom-call | flops 20000000000 | bytes 67108864 | tf_op jit(solution)/shard_map/attention/pallas_call | solution.py:612
  79.4 1.3 copy-done.18
  80.7 1.0 copy-done.20
  81.7 2.8 %collective-permute-start = (bf16[192,4096]{1,0:T(8,128)(2,1)S(1)}, bf16[192,4096]{1,0:T(8,128)(2,1)S(1)}, u32[]{:S(2)}, u32[]{:S(2)}) collective-permute-start(bf16[192,4096]{1,0:T(8,128)(2,1)S(1)} %get-tuple-element.32.grads_ref.own_ref), channel_id=1, source_target_pairs={{0,64},{16,80},{32,96},{48,112},{64,0},{80,16},{96,32},{112,48},{1... | collective-permute-start | bytes 4718600 | tf_op jit(solution)/shard_map/ppermute | solution.py:587
  84.6 20.7 %experts.1 = (bf16[4,2,2,96,192]{4,3,2,1,0:T(8,128)(2,1)S(1)}, bf16[2,384,192]{2,1,0:T(8,128)(2,1)S(1)}, bf16[768,1024]{1,0:T(8,128)(2,1)S(1)}) custom-call(s32[1]{0:T(128)} %bitcast.14.mine_ref, bf16[192,4096]{1,0:T(8,128)(2,1)} %get-tuple-element.31.rows_ref, bf16[192,4096]{1,0:T(8,128)(2,1)S(1)} %get-tuple-element.32.grads_ref.own_ref, ...), custom_call_target="tpu_custom_call" | custom-call | flops 10000000000 | bytes 4194304 | tf_op jit(solution)/shard_map/experts/pallas_call | solution.py:653
  105.3 35.2 %return.1 = (bf16[16,48,1024]{2,1,0:T(8,128)(2,1)S(1)}, bf16[4,2,2,96,192]{4,3,2,1,0:T(8,128)(2,1)S(1)}, bf16[384,192]{1,0:T(8,128)(2,1)S(1)}) custom-call(bf16[16,48,1024]{2,1,0:T(8,128)(2,1)S(1)} %bitcast.30, bf16[4,2,2,96,192]{4,3,2,1,0:T(8,128)(2,1)S(1)} %get-tuple-element.34.terms_ref, ...), custom_call_target="tpu_custom_call" | custom-call | bytes 67108864 | tf_op jit(solution)/shard_map/return/pallas_call | solution.py:673
  140.5 1.1 copy-done.6
  141.7 0.9 copy-done.12
  142.6 3.8 %down_terms.1 = bf16[384,4096]{1,0:T(8,128)(2,1)} custom-call(bf16[192,4096]{1,0:T(8,128)(2,1)S(1)} %get-tuple-element.32.grads_ref.own_ref, bf16[192,4096]{1,0:T(8,128)(2,1)S(1)} %collective-permute-done.other_ref, bf16[2,384,192]{2,1,0:T(8,128)(2,1)S(1)} %get-tuple-element.35.products_ref.own_products_ref, ...), custom_call_target="tpu_custom_call" | custom-call | flops 4000000000 | bytes 4194304 | tf_op jit(solution)/shard_map/down_terms/pallas_call | solution.py:689
  146.4 8.3 %all-gather.3.cloned.1.call-done = bf16[768,4096]{1,0:T(8,128)(2,1)} async-done(((bf16[192,4096]{1,0:T(8,128)(2,1)}), bf16[768,4096]{1,0:T(8,128)(2,1)}) %all-gather.3.cloned.1.call-update) | async-done | bytes 6291472 | tf_op jit(solution)/shard_map/all_gather | solution.py:648
  154.7 1.1 copy-done.13
  155.8 2.8 %copy-done.5 = bf16[768,4096]{1,0:T(8,128)(2,1)S(1)} copy-done((bf16[768,4096]{1,0:T(8,128)(2,1)S(1)}, bf16[768,4096]{1,0:T(8,128)(2,1)}, u32[]{:S(2)}) %copy-start.5) | copy-done | bytes 6291480
  158.6 4.5 %gate_up_terms.1 = (bf16[192,4096]{1,0:T(8,128)(2,1)S(1)}, bf16[192,4096]{1,0:T(8,128)(2,1)S(1)}) custom-call(bf16[4,2,2,96,192]{4,3,2,1,0:T(8,128)(2,1)S(1)} %copy-done.13, bf16[4,192,4096]{2,1,0:T(8,128)(2,1)S(1)} %bitcast.34), custom_call_target="tpu_custom_call" | custom-call | flops 4000000000 | bytes 4194304 | tf_op jit(solution)/shard_map/gate_up_terms/pallas_call | solution.py:706
  163.1 2.8 %collective-permute-start.1 = (bf16[192,4096]{1,0:T(8,128)(2,1)S(1)}, bf16[192,4096]{1,0:T(8,128)(2,1)S(1)}, u32[]{:S(2)}, u32[]{:S(2)}) collective-permute-start(bf16[192,4096]{1,0:T(8,128)(2,1)S(1)} %get-tuple-element.50), channel_id=1, source_target_pairs={{0,64},{16,80},{32,96},{48,112},{64,0},{80,16},{96,32},{112,48},{1... | collective-permute-start | bytes 4718600 | tf_op jit(solution)/shard_map/ppermute | solution.py:587
  166.0 14.2 %attention_grads_0.1 = (bf16[128,2048]{1,0:T(8,128)(2,1)S(1)}, bf16[2048,256]{1,0:T(8,128)(2,1)S(1)}, bf16[128,4096]{1,0:T(8,128)(2,1)S(1)}) custom-call(bf16[128,4096]{1,0:T(8,128)(2,1)S(1)} %bitcast.39, bf16[2048,512]{1,0:T(8,128)(2,1)S(1)} %bitcast.47, bf16[2048,128]{1,0:T(8,128)(2,1)S(1)} %copy-done.4, s32[8,128]{1,0:T(8,128)S(1)} %bitcast.46, ...), custom_call_target="tpu_custom_call" | custom-call | flops 20000000000 | bytes 4194304 | tf_op jit(solution)/shard_map/attention_grads_0/pallas_call | solution.py:727
  180.2 31.8 %attention_grads_1.1 = (bf16[128,4096]{1,0:T(8,128)(2,1)S(1)}, bf16[128,256]{1,0:T(8,128)(2,1)S(1)}, bf16[128,256]{1,0:T(8,128)(2,1)S(1)}) custom-call(bf16[128,4096]{1,0:T(8,128)(2,1)S(1)} %bitcast.40, bf16[2048,512]{1,0:T(8,128)(2,1)S(1)} %bitcast.48, bf16[2048,128]{1,0:T(8,128)(2,1)S(1)} %copy-done.4, bf16[128,4096]{1,0:T(8,128)(2,1)S(1)} %copy-done.21, ...), custom_call_target="tpu_custom_call" | custom-call | flops 20000000000 | bytes 67108864 | tf_op jit(solution)/shard_map/attention_grads_1/pallas_call | solution.py:739
  212.0 1.0 copy-done
  213.0 1.1 copy-done.2
  214.1 1.8 expert_grads.1
  215.9 1.0 copy.20
  216.9 0.6 copy.21
  217.5 0.6 copy.22
  (41 shorter events, 0.3 us)
Async XLA Ops:
  7.2 147.5 %all-gather.3.cloned.1.call-start = ((), (), s32[]{:S(2)}) async-start(), calls=%async_computation.2 | async-start | bytes 7864320 | tf_op jit(solution)/shard_map/all_gather | solution.py:648
  9.2 5.0 %copy-start.3 = (bf16[2048,128]{1,0:T(8,128)(2,1)}, bf16[2048,128]{1,0:T(8,128)(2,1)S(1)}, u32[]{:S(2)}) copy-start(bf16[2048,128]{1,0:T(8,128)(2,1)S(1)} %compare_convert_fusion.hidden_ref) | copy-start | bytes 1572868
  10.2 1.2 copy-start.8
  11.4 0.7 copy-start.15
  12.1 0.7 copy-start.16
  12.8 1.4 copy-start.10
  12.8 1.4 copy-start.14
  79.4 1.3 copy-start.18
  80.7 1.0 copy-start.20
  81.7 131.3 %reduce-scatter.2.cloned.1.call-start = ((), (), s32[]{:S(2)}) async-start(), calls=%async_computation.1 | async-start | bytes 3932160 | tf_op jit(solution)/shard_map/reduce_scatter | solution.py:702
  81.7 60.9 %collective-permute-start = (bf16[192,4096]{1,0:T(8,128)(2,1)S(1)}, bf16[192,4096]{1,0:T(8,128)(2,1)S(1)}, u32[]{:S(2)}, u32[]{:S(2)}) collective-permute-start(bf16[192,4096]{1,0:T(8,128)(2,1)S(1)} %get-tuple-element.32.grads_ref.own_ref), channel_id=1, source_target_pairs={{0,64},{16,80},{32,96},{48,112},{64,0},{80,16},{96,32},{112,48},{1... | collective-permute-start | bytes 4718600 | tf_op jit(solution)/shard_map/ppermute | solution.py:587
  140.5 1.2 copy-start.6
  141.7 0.9 copy-start.12
  154.6 1.1 copy-start.13
  155.8 2.8 %copy-start.5 = (bf16[768,4096]{1,0:T(8,128)(2,1)S(1)}, bf16[768,4096]{1,0:T(8,128)(2,1)}, u32[]{:S(2)}) copy-start(bf16[768,4096]{1,0:T(8,128)(2,1)} %all-gather.3.cloned.1.call-done) | copy-start | bytes 18874372
  158.6 7.4 %copy-start.4 = (bf16[2048,128]{1,0:T(8,128)(2,1)S(1)}, bf16[2048,128]{1,0:T(8,128)(2,1)}, u32[]{:S(2)}) copy-start(bf16[2048,128]{1,0:T(8,128)(2,1)} %copy-done.3) | copy-start | bytes 1572868
  158.6 7.4 %copy-start.7 = (bf16[16,48,1024]{2,1,0:T(8,128)(2,1)S(1)}, bf16[16,48,1024]{2,1,0:T(8,128)(2,1)}, u32[]{:S(2)}) copy-start(bf16[16,48,1024]{2,1,0:T(8,128)(2,1)} %copy-done.6) | copy-start | bytes 4718596
  158.6 7.4 %copy-start.9 = (bf16[1,128,4096]{2,1,0:T(8,128)(2,1)S(1)}, bf16[1,128,4096]{2,1,0:T(8,128)(2,1)}, u32[]{:S(2)}) copy-start(bf16[1,128,4096]{2,1,0:T(8,128)(2,1)} %param.18) | copy-start | bytes 3145732
  158.6 7.4 %copy-start.11 = (bf16[1,128,4096]{2,1,0:T(8,128)(2,1)S(1)}, bf16[1,128,4096]{2,1,0:T(8,128)(2,1)}, u32[]{:S(2)}) copy-start(bf16[1,128,4096]{2,1,0:T(8,128)(2,1)} %param.10) | copy-start | bytes 3145732
  158.6 7.4 %copy-start.17 = (s32[1,128,8]{1,2,0:T(8,128)S(1)}, s32[1,128,8]{1,2,0:T(8,128)}, u32[]{:S(2)}) copy-start(s32[1,128,8]{1,2,0:T(8,128)} %param.14) | copy-start | bytes 12292
  158.6 7.4 %copy-start.19 = (bf16[16,128,512]{2,1,0:T(8,128)(2,1)S(1)}, bf16[16,128,512]{2,1,0:T(8,128)(2,1)}, u32[]{:S(2)}) copy-start(bf16[16,128,512]{2,1,0:T(8,128)(2,1)} %copy-done.18) | copy-start | bytes 6291460
  158.6 7.4 %copy-start.21 = (bf16[128,4096]{1,0:T(8,128)(2,1)S(1)}, bf16[128,4096]{1,0:T(8,128)(2,1)}, u32[]{:S(2)}) copy-start(bf16[128,4096]{1,0:T(8,128)(2,1)} %copy-done.20) | copy-start | bytes 3145732
  163.1 49.9 %collective-permute-start.1 = (bf16[192,4096]{1,0:T(8,128)(2,1)S(1)}, bf16[192,4096]{1,0:T(8,128)(2,1)S(1)}, u32[]{:S(2)}, u32[]{:S(2)}) collective-permute-start(bf16[192,4096]{1,0:T(8,128)(2,1)S(1)} %get-tuple-element.50), channel_id=1, source_target_pairs={{0,64},{16,80},{32,96},{48,112},{64,0},{80,16},{96,32},{112,48},{1... | collective-permute-start | bytes 4718600 | tf_op jit(solution)/shard_map/ppermute | solution.py:587
  212.0 1.0 copy-start
  213.0 1.1 copy-start.2
  214.1 1.8 copy-start.1
Sparse Core Ops, SparseCore 0:
  81.8 72.7 all-gather.2
  157.1 38.9 reduce-scatter.1

commit v3 on v2

--- a/solution.py
+++ b/solution.py
@@ -180,6 +180,16 @@
     own = pltpu.make_async_copy(kv_ref, whole_ref.at[me], own_sem.at[0])
     own.start()
 
+    slabs = []
+    for d, other in enumerate(others):
+        copy = send(
+            slabs_ref.at[other], slabs_in.at[me], slab_send.at[d], slab_recv.at[d], other
+        )
+        copy.start()
+        slabs.append(copy)
+    own_slab = pltpu.make_async_copy(slabs_ref.at[me], slabs_in.at[me], own_sem.at[1])
+    own_slab.start()
+
     mask, _ = slot_mask(expert_ranks(ids_ref, trainable_ref), CAP)
     mask = jnp.where(mask, 1.0, 0.0).astype(BF)
     swap = swap_mask()
@@ -203,16 +213,6 @@
     own.wait()
     for copy in passed:
         copy.wait()
-
-    slabs = []
-    for d, other in enumerate(others):
-        copy = send(
-            slabs_ref.at[other], slabs_in.at[me], slab_send.at[d], slab_recv.at[d], other
-        )
-        copy.start()
-        slabs.append(copy)
-    own_slab = pltpu.make_async_copy(slabs_ref.at[me], slabs_in.at[me], own_sem.at[1])
-    own_slab.start()
 
     for g in range(KEY_VALUE_HEADS):
         at = g * HEAD_SIZE

time: 227 us -> 224 us (0.987)
  Pallas kernels: 179 us -> 173 us
    pallas_call x1, Pallas kernels: 65.2 us -> 59.8 us  [per_device(): pl.pallas_call(forward_kernel, out_shape=(bf_shape(N_CTX, ROWS, 2 * group...]
  transfers between devices with their start and end apart: 4 -> 4, of which waited for: 1 -> 1; matrix products, arithmetic and copies ran while one was open for 0% -> 0% of each run, Pallas kernels for 49% -> 50%
where the time goes in v3:
time: 224 us; the launch traced here: 221 us
  Pallas kernels  173 us (77%)
  local copies, waits for them, and re-layouts  16.1 us (7%)
  between operations  14.2 us (6%)
  waiting for transfers between devices  10.1 us (5%)
  starting transfers between devices  5.8 us (3%)
    pallas_call x1, Pallas kernels, per_device(): pl.pallas_call(forward_kernel, out_shape=(bf_shape(N_CTX, ROWS, 2 * group...  59.8 us
    pallas_call x1, Pallas kernels, per_device(): pl.pallas_call(return_kernel, out_shape=(bf_shape(*slabs), bf_shape(*term...  35.2 us
    pallas_call x1, Pallas kernels, per_device(): pl.pallas_call(second_backward_kernel, out_shape=(bf_shape(ROWS, D), *[bf...  31.7 us
    pallas_call x1, Pallas kernels, per_device(): pl.pallas_call(expert_kernel, out_shape=(bf_shape(*term_shape), bf_shape(...  20.7 us
    unnamed x47, local copies, waits for them, and re-layouts  15.2 us
    pallas_call x1, Pallas kernels, per_device(): pl.pallas_call(first_backward_kernel, out_shape=(bf_shape(ROWS, D // 2),...  14.2 us
    all_gather x1, waiting for transfers between devices, per_device(): all_rows = lax.all_gather(rows, 'dp', axis=0, axis_index_groups=X_GROUPS)  10.1 us
    ppermute x2, starting transfers between devices, over_pair(): return lax.ppermute(array, 'dp', [(i, (i + 4) % 8) for i in range(8)])  5.72 us
  transfers between devices with their start and end apart: 4, of which 1 were waited for; matrix products, arithmetic and copies ran while one was open for 0% of the time, Pallas kernels for 50%

profile of v3, /device:TPU:1, one launch (start us, length us, event | category | flops | bytes accessed | tf_op | source)
XLA Modules:
  0.0 221.4 jit_solution(16775461634360383092)
XLA Ops:
  7.2 0.7 copy.14.trainable_ref
  7.9 0.7 multiply_bitcast_fusion
  8.6 0.1 iota_add_fusion
  8.8 0.1 dynamic_slice.3
  8.8 0.3 compare_convert_fusion.hidden_ref
  9.2 1.0 pad_maximum_fusion.kv_ref
  10.2 1.2 copy-done.8
  11.4 0.7 copy-done.15
  12.1 0.7 copy-done.16
  12.8 1.3 weighted.1
  14.2 59.8 %attention.1 = (bf16[16,128,512]{2,1,0:T(8,128)(2,1)S(1)}, bf16[128,4096]{1,0:T(8,128)(2,1)S(1)}, f32[16,256]{1,0:T(8,128)S(1)}, bf16[192,4096]{1,0:T(8,128)(2,1)}, bf16[192,4096]{1,0:T(8,128)(2,1)S(1)}) custom-call(bf16[128,512]{1,0:T(8,128)(2,1)S(1)} %pad_maximum_fusion.kv_ref, bf16[16,48,1024]{2,1,0:T(8,128)(2,1)S(1)} %bitcast.49, ...), custom_call_target="tpu_custom_call" | custom-call | flops 20000000000 | bytes 67108864 | tf_op jit(solution)/shard_map/attention/pallas_call | solution.py:612
  74.0 1.3 copy-done.18
  75.4 1.0 copy-done.20
  76.4 2.9 %collective-permute-start = (bf16[192,4096]{1,0:T(8,128)(2,1)S(1)}, bf16[192,4096]{1,0:T(8,128)(2,1)S(1)}, u32[]{:S(2)}, u32[]{:S(2)}) collective-permute-start(bf16[192,4096]{1,0:T(8,128)(2,1)S(1)} %get-tuple-element.32.grads_ref.own_ref), channel_id=1, source_target_pairs={{0,64},{16,80},{32,96},{48,112},{64,0},{80,16},{96,32},{112,48},{1... | collective-permute-start | bytes 4718600 | tf_op jit(solution)/shard_map/ppermute | solution.py:587
  79.3 20.7 %experts.1 = (bf16[4,2,2,96,192]{4,3,2,1,0:T(8,128)(2,1)S(1)}, bf16[2,384,192]{2,1,0:T(8,128)(2,1)S(1)}, bf16[768,1024]{1,0:T(8,128)(2,1)S(1)}) custom-call(s32[1]{0:T(128)} %bitcast.14.mine_ref, bf16[192,4096]{1,0:T(8,128)(2,1)} %get-tuple-element.31.rows_ref, bf16[192,4096]{1,0:T(8,128)(2,1)S(1)} %get-tuple-element.32.grads_ref.own_ref, ...), custom_call_target="tpu_custom_call" | custom-call | flops 10000000000 | bytes 4194304 | tf_op jit(solution)/shard_map/experts/pallas_call | solution.py:653
  100.0 35.2 %return.1 = (bf16[16,48,1024]{2,1,0:T(8,128)(2,1)S(1)}, bf16[4,2,2,96,192]{4,3,2,1,0:T(8,128)(2,1)S(1)}, bf16[384,192]{1,0:T(8,128)(2,1)S(1)}) custom-call(bf16[16,48,1024]{2,1,0:T(8,128)(2,1)S(1)} %bitcast.30, bf16[4,2,2,96,192]{4,3,2,1,0:T(8,128)(2,1)S(1)} %get-tuple-element.34.terms_ref, ...), custom_call_target="tpu_custom_call" | custom-call | bytes 67108864 | tf_op jit(solution)/shard_map/return/pallas_call | solution.py:673
  135.2 1.1 copy-done.6
  136.3 0.9 copy-done.12
  137.3 3.8 %down_terms.1 = bf16[384,4096]{1,0:T(8,128)(2,1)} custom-call(bf16[192,4096]{1,0:T(8,128)(2,1)S(1)} %get-tuple-element.32.grads_ref.own_ref, bf16[192,4096]{1,0:T(8,128)(2,1)S(1)} %collective-permute-done.other_ref, bf16[2,384,192]{2,1,0:T(8,128)(2,1)S(1)} %get-tuple-element.35.products_ref.own_products_ref, ...), custom_call_target="tpu_custom_call" | custom-call | flops 4000000000 | bytes 4194304 | tf_op jit(solution)/shard_map/down_terms/pallas_call | solution.py:689
  141.0 10.1 %all-gather.3.cloned.1.call-done = bf16[768,4096]{1,0:T(8,128)(2,1)} async-done(((bf16[192,4096]{1,0:T(8,128)(2,1)}), bf16[768,4096]{1,0:T(8,128)(2,1)}) %all-gather.3.cloned.1.call-update) | async-done | bytes 6291472 | tf_op jit(solution)/shard_map/all_gather | solution.py:648
  151.2 1.1 copy-done.13
  152.3 2.8 %copy-done.5 = bf16[768,4096]{1,0:T(8,128)(2,1)S(1)} copy-done((bf16[768,4096]{1,0:T(8,128)(2,1)S(1)}, bf16[768,4096]{1,0:T(8,128)(2,1)}, u32[]{:S(2)}) %copy-start.5) | copy-done | bytes 6291480
  155.1 4.5 %gate_up_terms.1 = (bf16[192,4096]{1,0:T(8,128)(2,1)S(1)}, bf16[192,4096]{1,0:T(8,128)(2,1)S(1)}) custom-call(bf16[4,2,2,96,192]{4,3,2,1,0:T(8,128)(2,1)S(1)} %copy-done.13, bf16[4,192,4096]{2,1,0:T(8,128)(2,1)S(1)} %bitcast.34), custom_call_target="tpu_custom_call" | custom-call | flops 4000000000 | bytes 4194304 | tf_op jit(solution)/shard_map/gate_up_terms/pallas_call | solution.py:706
  159.6 2.8 %collective-permute-start.1 = (bf16[192,4096]{1,0:T(8,128)(2,1)S(1)}, bf16[192,4096]{1,0:T(8,128)(2,1)S(1)}, u32[]{:S(2)}, u32[]{:S(2)}) collective-permute-start(bf16[192,4096]{1,0:T(8,128)(2,1)S(1)} %get-tuple-element.50), channel_id=1, source_target_pairs={{0,64},{16,80},{32,96},{48,112},{64,0},{80,16},{96,32},{112,48},{1... | collective-permute-start | bytes 4718600 | tf_op jit(solution)/shard_map/ppermute | solution.py:587
  162.5 14.2 %attention_grads_0.1 = (bf16[128,2048]{1,0:T(8,128)(2,1)S(1)}, bf16[2048,256]{1,0:T(8,128)(2,1)S(1)}, bf16[128,4096]{1,0:T(8,128)(2,1)S(1)}) custom-call(bf16[128,4096]{1,0:T(8,128)(2,1)S(1)} %bitcast.39, bf16[2048,512]{1,0:T(8,128)(2,1)S(1)} %bitcast.47, bf16[2048,128]{1,0:T(8,128)(2,1)S(1)} %copy-done.4, s32[8,128]{1,0:T(8,128)S(1)} %bitcast.46, ...), custom_call_target="tpu_custom_call" | custom-call | flops 20000000000 | bytes 4194304 | tf_op jit(solution)/shard_map/attention_grads_0/pallas_call | solution.py:727
  176.7 31.7 %attention_grads_1.1 = (bf16[128,4096]{1,0:T(8,128)(2,1)S(1)}, bf16[128,256]{1,0:T(8,128)(2,1)S(1)}, bf16[128,256]{1,0:T(8,128)(2,1)S(1)}) custom-call(bf16[128,4096]{1,0:T(8,128)(2,1)S(1)} %bitcast.40, bf16[2048,512]{1,0:T(8,128)(2,1)S(1)} %bitcast.48, bf16[2048,128]{1,0:T(8,128)(2,1)S(1)} %copy-done.4, bf16[128,4096]{1,0:T(8,128)(2,1)S(1)} %copy-done.21, ...), custom_call_target="tpu_custom_call" | custom-call | flops 20000000000 | bytes 67108864 | tf_op jit(solution)/shard_map/attention_grads_1/pallas_call | solution.py:739
  208.5 1.0 copy-done
  209.4 1.1 copy-done.2
  210.6 1.8 expert_grads.1
  212.4 1.0 copy.20
  213.3 0.6 copy.21
  214.0 0.6 copy.22
  (41 shorter events, 0.3 us)
Async XLA Ops:
  7.2 144.0 %all-gather.3.cloned.1.call-start = ((), (), s32[]{:S(2)}) async-start(), calls=%async_computation.2 | async-start | bytes 7864320 | tf_op jit(solution)/shard_map/all_gather | solution.py:648
  9.2 5.0 %copy-start.3 = (bf16[2048,128]{1,0:T(8,128)(2,1)}, bf16[2048,128]{1,0:T(8,128)(2,1)S(1)}, u32[]{:S(2)}) copy-start(bf16[2048,128]{1,0:T(8,128)(2,1)S(1)} %compare_convert_fusion.hidden_ref) | copy-start | bytes 1572868
  10.2 1.2 copy-start.8
  11.4 0.7 copy-start.15
  12.1 0.7 copy-start.16
  12.8 1.4 copy-start.10
  12.8 1.4 copy-start.14
  74.0 1.3 copy-start.18
  75.4 1.0 copy-start.20
  76.4 133.1 %reduce-scatter.2.cloned.1.call-start = ((), (), s32[]{:S(2)}) async-start(), calls=%async_computation.1 | async-start | bytes 3932160 | tf_op jit(solution)/shard_map/reduce_scatter | solution.py:702
  76.4 60.9 %collective-permute-start = (bf16[192,4096]{1,0:T(8,128)(2,1)S(1)}, bf16[192,4096]{1,0:T(8,128)(2,1)S(1)}, u32[]{:S(2)}, u32[]{:S(2)}) collective-permute-start(bf16[192,4096]{1,0:T(8,128)(2,1)S(1)} %get-tuple-element.32.grads_ref.own_ref), channel_id=1, source_target_pairs={{0,64},{16,80},{32,96},{48,112},{64,0},{80,16},{96,32},{112,48},{1... | collective-permute-start | bytes 4718600 | tf_op jit(solution)/shard_map/ppermute | solution.py:587
  135.2 1.2 copy-start.6
  136.3 0.9 copy-start.12
  151.1 1.1 copy-start.13
  152.3 2.8 %copy-start.5 = (bf16[768,4096]{1,0:T(8,128)(2,1)S(1)}, bf16[768,4096]{1,0:T(8,128)(2,1)}, u32[]{:S(2)}) copy-start(bf16[768,4096]{1,0:T(8,128)(2,1)} %all-gather.3.cloned.1.call-done) | copy-start | bytes 18874372
  155.0 7.4 %copy-start.4 = (bf16[2048,128]{1,0:T(8,128)(2,1)S(1)}, bf16[2048,128]{1,0:T(8,128)(2,1)}, u32[]{:S(2)}) copy-start(bf16[2048,128]{1,0:T(8,128)(2,1)} %copy-done.3) | copy-start | bytes 1572868
  155.0 7.4 %copy-start.7 = (bf16[16,48,1024]{2,1,0:T(8,128)(2,1)S(1)}, bf16[16,48,1024]{2,1,0:T(8,128)(2,1)}, u32[]{:S(2)}) copy-start(bf16[16,48,1024]{2,1,0:T(8,128)(2,1)} %copy-done.6) | copy-start | bytes 4718596
  155.1 7.4 %copy-start.9 = (bf16[1,128,4096]{2,1,0:T(8,128)(2,1)S(1)}, bf16[1,128,4096]{2,1,0:T(8,128)(2,1)}, u32[]{:S(2)}) copy-start(bf16[1,128,4096]{2,1,0:T(8,128)(2,1)} %param.18) | copy-start | bytes 3145732
  155.1 7.4 %copy-start.11 = (bf16[1,128,4096]{2,1,0:T(8,128)(2,1)S(1)}, bf16[1,128,4096]{2,1,0:T(8,128)(2,1)}, u32[]{:S(2)}) copy-start(bf16[1,128,4096]{2,1,0:T(8,128)(2,1)} %param.10) | copy-start | bytes 3145732
  155.1 7.4 %copy-start.17 = (s32[1,128,8]{1,2,0:T(8,128)S(1)}, s32[1,128,8]{1,2,0:T(8,128)}, u32[]{:S(2)}) copy-start(s32[1,128,8]{1,2,0:T(8,128)} %param.14) | copy-start | bytes 12292
  155.1 7.4 %copy-start.19 = (bf16[16,128,512]{2,1,0:T(8,128)(2,1)S(1)}, bf16[16,128,512]{2,1,0:T(8,128)(2,1)}, u32[]{:S(2)}) copy-start(bf16[16,128,512]{2,1,0:T(8,128)(2,1)} %copy-done.18) | copy-start | bytes 6291460
  155.1 7.4 %copy-start.21 = (bf16[128,4096]{1,0:T(8,128)(2,1)S(1)}, bf16[128,4096]{1,0:T(8,128)(2,1)}, u32[]{:S(2)}) copy-start(bf16[128,4096]{1,0:T(8,128)(2,1)} %copy-done.20) | copy-start | bytes 3145732
  159.6 49.8 %collective-permute-start.1 = (bf16[192,4096]{1,0:T(8,128)(2,1)S(1)}, bf16[192,4096]{1,0:T(8,128)(2,1)S(1)}, u32[]{:S(2)}, u32[]{:S(2)}) collective-permute-start(bf16[192,4096]{1,0:T(8,128)(2,1)S(1)} %get-tuple-element.50), channel_id=1, source_target_pairs={{0,64},{16,80},{32,96},{48,112},{64,0},{80,16},{96,32},{112,48},{1... | collective-permute-start | bytes 4718600 | tf_op jit(solution)/shard_map/ppermute | solution.py:587
  208.5 1.0 copy-start
  209.4 1.1 copy-start.2
  210.6 1.8 copy-start.1
Sparse Core Ops, SparseCore 0:
  76.5 74.6 all-gather.2
  153.5 38.9 reduce-scatter.1
